TPU v7x, 32 devices: a whole 2x2x4 slice. The times are simulated.
32 devices in a mesh: win: 2 (over x), row: 4 (over y, core), col: 4 (over z).
Axes of the slice: x: 2, y: 2, z: 4, core: 2. Of those that a mesh axis runs over, the one named last changes fastest.
Arguments:
- left_blocks: bfloat16 [16, 16, 16, 9216], P(('win', 'col'), 'row'), parts along dimension 0, may hold values from -0.15625 to 0.15625
- right_blocks: bfloat16 [16, 16, 16, 9216], P(('win', 'col'), 'row'), parts along dimension 0, may hold values from -12 to 12
- pattern: int32 [16, 16, 16], P(('win', 'col'), 'row'), parts along dimension 0, may hold values from 0 to 127, as said below
- left_live: int32 [16, 16, 16], P(('win', 'col'), 'row'), parts along dimension 0, may hold values from 0 to 1, as said below
- right_live: int32 [16, 16, 16], P(('win', 'col'), 'row'), parts along dimension 0, may hold values from 0 to 1, as said below
Outputs:
- next_iterate: bfloat16 [16, 16, 16, 9216], P(('win', 'col'), 'row'), parts along dimension 0
There are 2 independent parts, one for each index of `win`. A program takes and returns all parts, laid end to end along the dimension named above; each array names one. Nothing has to cross between parts.
Inputs may be any that keep to these rules, and one draw needn't show every extreme that they name: Block row i = 16 x + y sits at cell (x, y) of a periodic 8 x 16 grid. pattern[x, y, 0] = i; the other 15 entries are distinct cells (x', y') other than (x, y), given as 16 x' + y', with x' - x and y' - y in -2 to 2 modulo 8 and 16. `left_live`: 1 marks a tile that the filter keeps. `right_live`: 1 marks a tile that the filter keeps.
All inputs are finite; a program needn't handle non-finite values.
Results may differ from a plain program's by a relative error of at most 0.001.
Values may be sent and summed in bfloat16 or wider, within the bound.
A program may use at most 128 MiB of HBM per device.

v0:
```python
import jax
import jax.numpy as jnp
from jax import lax
from jax.sharding import PartitionSpec as P

BS = 96


def padded(array, sides, width):
    for axis, dim in sides:
        peers, length = (lax.axis_size(axis), array.shape[dim])
        up = [(i, (i + 1) % peers) for i in range(peers)]
        down = [(j, i) for i, j in up]
        last = lax.slice_in_dim(array, length - width, length, axis=dim)
        initial = lax.slice_in_dim(array, 0, width, axis=dim)
        before = lax.ppermute(last, axis, up)
        after = lax.ppermute(initial, axis, down)
        array = jnp.concatenate([before, array, after], axis=dim)
    return array


def body(left_blocks, right_blocks, pattern, left_live, right_live):
    cells_x, cells_y, slot_count, tile_area = left_blocks.shape
    near_tiles, near_pattern, near_live = (
        padded(right_blocks, (("col", 0), ("row", 1)), 2),
        padded(pattern, (("col", 0), ("row", 1)), 2),
        padded(right_live, (("col", 0), ("row", 1)), 2),
    )
    halo_y = cells_y + 4
    grid_x = cells_x * lax.axis_size("col")
    grid_y = cells_y * lax.axis_size("row")
    local_x = jnp.arange(cells_x, dtype=jnp.int32)[:, None, None]
    local_y = jnp.arange(cells_y, dtype=jnp.int32)[None, :, None]
    own_x = lax.axis_index("col") * cells_x + local_x
    own_y = lax.axis_index("row") * cells_y + local_y
    step_x = (pattern // grid_y - own_x + 2) % grid_x - 2
    step_y = (pattern % grid_y - own_y + 2) % grid_y - 2
    rows_here = cells_x * cells_y
    place = ((local_x + 2 + step_x) * halo_y + (local_y + 2 + step_y)).reshape(
        rows_here, slot_count
    )
    flat_tiles = near_tiles.reshape(-1, slot_count, tile_area)
    flat_pattern = near_pattern.reshape(-1, slot_count)
    flat_live = near_live.reshape(-1, slot_count)
    left_mask = left_live.reshape(rows_here, slot_count).astype(jnp.bfloat16)
    left_tiles = left_blocks.reshape(rows_here, slot_count, tile_area) * left_mask[:, :, None]
    left_tiles = jnp.moveaxis(left_tiles.reshape(rows_here, slot_count, BS, BS), 1, 0)
    targets = pattern.reshape(rows_here, slot_count)
    place_turns = jnp.moveaxis(place, 1, 0)

    def add_group(running, inputs):
        rows_at, left_group = inputs
        source_tiles = flat_tiles[rows_at]
        source_cols = flat_pattern[rows_at]
        source_live = flat_live[rows_at]
        select = (source_cols[:, None, :] == targets[:, :, None]).astype(
            jnp.bfloat16
        ) * source_live[:, None, :].astype(jnp.bfloat16)
        picked = jnp.einsum(
            "rqs,rsn->rqn", select, source_tiles, preferred_element_type=jnp.float32
        ).astype(jnp.bfloat16)
        picked = picked.reshape(rows_here, slot_count, BS, BS)
        return (
            running
            + jnp.einsum("rab,rqbc->rqac", left_group, picked, preferred_element_type=jnp.float32),
            None,
        )

    start_sum = jnp.zeros((rows_here, slot_count, BS, BS), jnp.float32)
    total, unused_out = lax.scan(add_group, start_sum, (place_turns, left_tiles))
    results = (0.5 * total).astype(jnp.bfloat16)
    return results.reshape(cells_x, cells_y, slot_count, tile_area)


def solution(mesh):
    placed = (
        P(("win", "col"), "row", None, None),
        P(("win", "col"), "row", None, None),
        P(("win", "col"), "row", None),
        P(("win", "col"), "row", None),
        P(("win", "col"), "row", None),
    )
    return jax.shard_map(
        body,
        mesh=mesh,
        in_specs=placed,
        out_specs=P(("win", "col"), "row", None, None),
        check_vma=False,
    )
```

profile of v0, /device:TPU:0, one launch (start us, length us, event | category | flops | bytes accessed | tf_op | source)
XLA Modules:
  0.0 541.1 jit_solution(5653023436248732085)
XLA Ops:
  5.1 52.4 %collective-permute-done.8 = bf16[2,4,16,9216]{3,2,1,0:T(8,128)(2,1)S(1)} collective-permute-done((bf16[2,4,16,9216]{3,2,1,0:T(8,128)(2,1)}, bf16[2,4,16,9216]{3,2,1,0:T(8,128)(2,1)S(1)}, u32[]{:S(2)}, u32[]{:S(2)}) %collective-permute-start.8) | collective-permute-done | bytes 2359328 | tf_op jit(solution)/shard_map/ppermute | solution.py:16
  57.8 48.7 %collective-permute-done.9 = bf16[2,4,16,9216]{3,2,1,0:T(8,128)(2,1)S(1)} collective-permute-done((bf16[2,4,16,9216]{3,2,1,0:T(8,128)(2,1)}, bf16[2,4,16,9216]{3,2,1,0:T(8,128)(2,1)S(1)}, u32[]{:S(2)}, u32[]{:S(2)}) %collective-permute-start.9) | collective-permute-done | bytes 2359328 | tf_op jit(solution)/shard_map/ppermute | solution.py:17
  120.9 4.9 reshape.88
  133.7 55.6 %collective-permute-done.2 = s32[6,2,16]{2,1,0:T(2,128)S(1)} collective-permute-done((s32[6,2,16]{2,1,0:T(2,128)S(1)}, s32[6,2,16]{2,1,0:T(2,128)S(1)}, u32[]{:S(2)}, u32[]{:S(2)}) %collective-permute-start.2) | collective-permute-done | bytes 800 | tf_op jit(solution)/shard_map/ppermute | solution.py:16
  190.7 12.4 %pad_maximum_fusion = bf16[6,8,16,9216]{3,2,1,0:T(8,128)(2,1)} fusion(bf16[6,2,16,9216]{3,2,1,0:T(8,128)(2,1)} %collective-permute-done.11, bf16[6,4,16,9216]{3,2,1,0:T(8,128)(2,1)} %copy-done, bf16[6,2,16,9216]{3,2,1,0:T(8,128)(2,1)} %collective-permute-done.10), kind=kLoop, calls=%fused_computation.17 | loop fusion | flops 14155776 | bytes 28311552 | tf_op jit(solution)/shard_map/concatenate | solution.py:18
  203.1 324.9 %while.11 = (s32[]{:T(128)}, f32[8,16,96,96]{2,3,1,0:T(8,128)}, s32[16,8]{1,0:T(8,128)S(1)}, s32[48,16]{1,0:T(8,128)S(1)}, s32[2,4,16]{2,1,0:T(4,128)S(1)}, /*in...) while((s32[]{:T(128)}, f32[8,16,96,96]{2,3,1,0:T(8,128)}, ...), condition=%wide.region_1.2_spmd.clone, body=%wide.region_0.1_spmd.clone.sunk | while | flops 267785376 | bytes 27730740 | solution.py:70
  203.1 5.7 %gather_fusion = bf16[8,16,9216]{2,1,0:T(8,128)(2,1)S(1)} fusion(bf16[48,16,9216]{2,1,0:T(8,128)(2,1)} %get-tuple-element.186, s32[1024]{0:T(1024)S(1)} %pad_clamp_fusion.2), kind=kCustom, calls=%fused_computation.2.clone.clone.1 | custom fusion | bytes 4718624 | tf_op jit(solution)/shard_map/while/body/eval_jaxpr/gather | solution.py:53
  212.2 4.5 reshape.136
  216.7 4.9 bitcast_add_fusion.2
  221.6 5.7 %gather_fusion = bf16[8,16,9216]{2,1,0:T(8,128)(2,1)S(1)} fusion(bf16[48,16,9216]{2,1,0:T(8,128)(2,1)} %get-tuple-element.186, s32[1024]{0:T(1024)S(1)} %pad_clamp_fusion.2), kind=kCustom, calls=%fused_computation.2.clone.clone.1 | custom fusion | bytes 4718624 | tf_op jit(solution)/shard_map/while/body/eval_jaxpr/gather | solution.py:53
  230.7 4.5 reshape.136
  235.1 6.8 %bitcast_add_fusion.2 = f32[8,16,96,96]{2,3,1,0:T(8,128)} fusion(f32[8,16,96,96]{2,3,1,0:T(8,128)} %get-tuple-element.171, pred[]{:T(512)S(6)} %compare.8, bf16[8,16,96,96]{3,2,1,0:T(8,128)(2,1)S(1)} %reshape.136, bf16[16,8,96,96]{3,2,1,0:T(8,128)(2,1)} %get-tuple-element.187, s32[]{:T(128)} %get-tuple-element.170), kind=kOutput, calls=%fused_computation.4.clone.1 | convolution fusion | flops 228851712 | bytes 13566465 | tf_op jit(solution)/shard_map/while/body/eval_jaxpr/rab,rqbc->rqac/dot_general | solution.py:65
  242.0 5.7 %gather_fusion = bf16[8,16,9216]{2,1,0:T(8,128)(2,1)S(1)} fusion(bf16[48,16,9216]{2,1,0:T(8,128)(2,1)} %get-tuple-element.186, s32[1024]{0:T(1024)S(1)} %pad_clamp_fusion.2), kind=kCustom, calls=%fused_computation.2.clone.clone.1 | custom fusion | bytes 4718624 | tf_op jit(solution)/shard_map/while/body/eval_jaxpr/gather | solution.py:53
  251.1 4.5 reshape.136
  255.6 6.8 %bitcast_add_fusion.2 = f32[8,16,96,96]{2,3,1,0:T(8,128)} fusion(f32[8,16,96,96]{2,3,1,0:T(8,128)} %get-tuple-element.171, pred[]{:T(512)S(6)} %compare.8, bf16[8,16,96,96]{3,2,1,0:T(8,128)(2,1)S(1)} %reshape.136, bf16[16,8,96,96]{3,2,1,0:T(8,128)(2,1)} %get-tuple-element.187, s32[]{:T(128)} %get-tuple-element.170), kind=kOutput, calls=%fused_computation.4.clone.1 | convolution fusion | flops 228851712 | bytes 13566465 | tf_op jit(solution)/shard_map/while/body/eval_jaxpr/rab,rqbc->rqac/dot_general | solution.py:65
  262.5 5.7 %gather_fusion = bf16[8,16,9216]{2,1,0:T(8,128)(2,1)S(1)} fusion(bf16[48,16,9216]{2,1,0:T(8,128)(2,1)} %get-tuple-element.186, s32[1024]{0:T(1024)S(1)} %pad_clamp_fusion.2), kind=kCustom, calls=%fused_computation.2.clone.clone.1 | custom fusion | bytes 4718624 | tf_op jit(solution)/shard_map/while/body/eval_jaxpr/gather | solution.py:53
  271.5 4.5 reshape.136
  276.0 6.8 %bitcast_add_fusion.2 = f32[8,16,96,96]{2,3,1,0:T(8,128)} fusion(f32[8,16,96,96]{2,3,1,0:T(8,128)} %get-tuple-element.171, pred[]{:T(512)S(6)} %compare.8, bf16[8,16,96,96]{3,2,1,0:T(8,128)(2,1)S(1)} %reshape.136, bf16[16,8,96,96]{3,2,1,0:T(8,128)(2,1)} %get-tuple-element.187, s32[]{:T(128)} %get-tuple-element.170), kind=kOutput, calls=%fused_computation.4.clone.1 | convolution fusion | flops 228851712 | bytes 13566465 | tf_op jit(solution)/shard_map/while/body/eval_jaxpr/rab,rqbc->rqac/dot_general | solution.py:65
  282.9 5.7 %gather_fusion = bf16[8,16,9216]{2,1,0:T(8,128)(2,1)S(1)} fusion(bf16[48,16,9216]{2,1,0:T(8,128)(2,1)} %get-tuple-element.186, s32[1024]{0:T(1024)S(1)} %pad_clamp_fusion.2), kind=kCustom, calls=%fused_computation.2.clone.clone.1 | custom fusion | bytes 4718624 | tf_op jit(solution)/shard_map/while/body/eval_jaxpr/gather | solution.py:53
  296.4 6.8 %bitcast_add_fusion.2 = f32[8,16,96,96]{2,3,1,0:T(8,128)} fusion(f32[8,16,96,96]{2,3,1,0:T(8,128)} %get-tuple-element.171, pred[]{:T(512)S(6)} %compare.8, bf16[8,16,96,96]{3,2,1,0:T(8,128)(2,1)S(1)} %reshape.136, bf16[16,8,96,96]{3,2,1,0:T(8,128)(2,1)} %get-tuple-element.187, s32[]{:T(128)} %get-tuple-element.170), kind=kOutput, calls=%fused_computation.4.clone.1 | convolution fusion | flops 228851712 | bytes 13566465 | tf_op jit(solution)/shard_map/while/body/eval_jaxpr/rab,rqbc->rqac/dot_general | solution.py:65
  303.3 5.7 %gather_fusion = bf16[8,16,9216]{2,1,0:T(8,128)(2,1)S(1)} fusion(bf16[48,16,9216]{2,1,0:T(8,128)(2,1)} %get-tuple-element.186, s32[1024]{0:T(1024)S(1)} %pad_clamp_fusion.2), kind=kCustom, calls=%fused_computation.2.clone.clone.1 | custom fusion | bytes 4718624 | tf_op jit(solution)/shard_map/while/body/eval_jaxpr/gather | solution.py:53
  312.4 4.5 reshape.136
  316.9 6.8 %bitcast_add_fusion.2 = f32[8,16,96,96]{2,3,1,0:T(8,128)} fusion(f32[8,16,96,96]{2,3,1,0:T(8,128)} %get-tuple-element.171, pred[]{:T(512)S(6)} %compare.8, bf16[8,16,96,96]{3,2,1,0:T(8,128)(2,1)S(1)} %reshape.136, bf16[16,8,96,96]{3,2,1,0:T(8,128)(2,1)} %get-tuple-element.187, s32[]{:T(128)} %get-tuple-element.170), kind=kOutput, calls=%fused_computation.4.clone.1 | convolution fusion | flops 228851712 | bytes 13566465 | tf_op jit(solution)/shard_map/while/body/eval_jaxpr/rab,rqbc->rqac/dot_general | solution.py:65
  323.7 5.7 %gather_fusion = bf16[8,16,9216]{2,1,0:T(8,128)(2,1)S(1)} fusion(bf16[48,16,9216]{2,1,0:T(8,128)(2,1)} %get-tuple-element.186, s32[1024]{0:T(1024)S(1)} %pad_clamp_fusion.2), kind=kCustom, calls=%fused_computation.2.clone.clone.1 | custom fusion | bytes 4718624 | tf_op jit(solution)/shard_map/while/body/eval_jaxpr/gather | solution.py:53
  332.8 4.5 reshape.136
  337.3 6.8 %bitcast_add_fusion.2 = f32[8,16,96,96]{2,3,1,0:T(8,128)} fusion(f32[8,16,96,96]{2,3,1,0:T(8,128)} %get-tuple-element.171, pred[]{:T(512)S(6)} %compare.8, bf16[8,16,96,96]{3,2,1,0:T(8,128)(2,1)S(1)} %reshape.136, bf16[16,8,96,96]{3,2,1,0:T(8,128)(2,1)} %get-tuple-element.187, s32[]{:T(128)} %get-tuple-element.170), kind=kOutput, calls=%fused_computation.4.clone.1 | convolution fusion | flops 228851712 | bytes 13566465 | tf_op jit(solution)/shard_map/while/body/eval_jaxpr/rab,rqbc->rqac/dot_general | solution.py:65
  344.2 5.7 %gather_fusion = bf16[8,16,9216]{2,1,0:T(8,128)(2,1)S(1)} fusion(bf16[48,16,9216]{2,1,0:T(8,128)(2,1)} %get-tuple-element.186, s32[1024]{0:T(1024)S(1)} %pad_clamp_fusion.2), kind=kCustom, calls=%fused_computation.2.clone.clone.1 | custom fusion | bytes 4718624 | tf_op jit(solution)/shard_map/while/body/eval_jaxpr/gather | solution.py:53
  353.3 4.5 reshape.136
  357.7 6.8 %bitcast_add_fusion.2 = f32[8,16,96,96]{2,3,1,0:T(8,128)} fusion(f32[8,16,96,96]{2,3,1,0:T(8,128)} %get-tuple-element.171, pred[]{:T(512)S(6)} %compare.8, bf16[8,16,96,96]{3,2,1,0:T(8,128)(2,1)S(1)} %reshape.136, bf16[16,8,96,96]{3,2,1,0:T(8,128)(2,1)} %get-tuple-element.187, s32[]{:T(128)} %get-tuple-element.170), kind=kOutput, calls=%fused_computation.4.clone.1 | convolution fusion | flops 228851712 | bytes 13566465 | tf_op jit(solution)/shard_map/while/body/eval_jaxpr/rab,rqbc->rqac/dot_general | solution.py:65
  364.6 5.7 %gather_fusion = bf16[8,16,9216]{2,1,0:T(8,128)(2,1)S(1)} fusion(bf16[48,16,9216]{2,1,0:T(8,128)(2,1)} %get-tuple-element.186, s32[1024]{0:T(1024)S(1)} %pad_clamp_fusion.2), kind=kCustom, calls=%fused_computation.2.clone.clone.1 | custom fusion | bytes 4718624 | tf_op jit(solution)/shard_map/while/body/eval_jaxpr/gather | solution.py:53
  373.7 4.5 reshape.136
  378.2 6.8 %bitcast_add_fusion.2 = f32[8,16,96,96]{2,3,1,0:T(8,128)} fusion(f32[8,16,96,96]{2,3,1,0:T(8,128)} %get-tuple-element.171, pred[]{:T(512)S(6)} %compare.8, bf16[8,16,96,96]{3,2,1,0:T(8,128)(2,1)S(1)} %reshape.136, bf16[16,8,96,96]{3,2,1,0:T(8,128)(2,1)} %get-tuple-element.187, s32[]{:T(128)} %get-tuple-element.170), kind=kOutput, calls=%fused_computation.4.clone.1 | convolution fusion | flops 228851712 | bytes 13566465 | tf_op jit(solution)/shard_map/while/body/eval_jaxpr/rab,rqbc->rqac/dot_general | solution.py:65
  385.0 5.7 %gather_fusion = bf16[8,16,9216]{2,1,0:T(8,128)(2,1)S(1)} fusion(bf16[48,16,9216]{2,1,0:T(8,128)(2,1)} %get-tuple-element.186, s32[1024]{0:T(1024)S(1)} %pad_clamp_fusion.2), kind=kCustom, calls=%fused_computation.2.clone.clone.1 | custom fusion | bytes 4718624 | tf_op jit(solution)/shard_map/while/body/eval_jaxpr/gather | solution.py:53
  394.1 4.5 reshape.136
  398.6 6.8 %bitcast_add_fusion.2 = f32[8,16,96,96]{2,3,1,0:T(8,128)} fusion(f32[8,16,96,96]{2,3,1,0:T(8,128)} %get-tuple-element.171, pred[]{:T(512)S(6)} %compare.8, bf16[8,16,96,96]{3,2,1,0:T(8,128)(2,1)S(1)} %reshape.136, bf16[16,8,96,96]{3,2,1,0:T(8,128)(2,1)} %get-tuple-element.187, s32[]{:T(128)} %get-tuple-element.170), kind=kOutput, calls=%fused_computation.4.clone.1 | convolution fusion | flops 228851712 | bytes 13566465 | tf_op jit(solution)/shard_map/while/body/eval_jaxpr/rab,rqbc->rqac/dot_general | solution.py:65
  405.5 5.7 %gather_fusion = bf16[8,16,9216]{2,1,0:T(8,128)(2,1)S(1)} fusion(bf16[48,16,9216]{2,1,0:T(8,128)(2,1)} %get-tuple-element.186, s32[1024]{0:T(1024)S(1)} %pad_clamp_fusion.2), kind=kCustom, calls=%fused_computation.2.clone.clone.1 | custom fusion | bytes 4718624 | tf_op jit(solution)/shard_map/while/body/eval_jaxpr/gather | solution.py:53
  419.0 6.8 %bitcast_add_fusion.2 = f32[8,16,96,96]{2,3,1,0:T(8,128)} fusion(f32[8,16,96,96]{2,3,1,0:T(8,128)} %get-tuple-element.171, pred[]{:T(512)S(6)} %compare.8, bf16[8,16,96,96]{3,2,1,0:T(8,128)(2,1)S(1)} %reshape.136, bf16[16,8,96,96]{3,2,1,0:T(8,128)(2,1)} %get-tuple-element.187, s32[]{:T(128)} %get-tuple-element.170), kind=kOutput, calls=%fused_computation.4.clone.1 | convolution fusion | flops 228851712 | bytes 13566465 | tf_op jit(solution)/shard_map/while/body/eval_jaxpr/rab,rqbc->rqac/dot_general | solution.py:65
  425.9 5.7 %gather_fusion = bf16[8,16,9216]{2,1,0:T(8,128)(2,1)S(1)} fusion(bf16[48,16,9216]{2,1,0:T(8,128)(2,1)} %get-tuple-element.186, s32[1024]{0:T(1024)S(1)} %pad_clamp_fusion.2), kind=kCustom, calls=%fused_computation.2.clone.clone.1 | custom fusion | bytes 4718624 | tf_op jit(solution)/shard_map/while/body/eval_jaxpr/gather | solution.py:53
  439.5 6.8 %bitcast_add_fusion.2 = f32[8,16,96,96]{2,3,1,0:T(8,128)} fusion(f32[8,16,96,96]{2,3,1,0:T(8,128)} %get-tuple-element.171, pred[]{:T(512)S(6)} %compare.8, bf16[8,16,96,96]{3,2,1,0:T(8,128)(2,1)S(1)} %reshape.136, bf16[16,8,96,96]{3,2,1,0:T(8,128)(2,1)} %get-tuple-element.187, s32[]{:T(128)} %get-tuple-element.170), kind=kOutput, calls=%fused_computation.4.clone.1 | convolution fusion | flops 228851712 | bytes 13566465 | tf_op jit(solution)/shard_map/while/body/eval_jaxpr/rab,rqbc->rqac/dot_general | solution.py:65
  446.3 5.7 %gather_fusion = bf16[8,16,9216]{2,1,0:T(8,128)(2,1)S(1)} fusion(bf16[48,16,9216]{2,1,0:T(8,128)(2,1)} %get-tuple-element.186, s32[1024]{0:T(1024)S(1)} %pad_clamp_fusion.2), kind=kCustom, calls=%fused_computation.2.clone.clone.1 | custom fusion | bytes 4718624 | tf_op jit(solution)/shard_map/while/body/eval_jaxpr/gather | solution.py:53
  459.9 6.8 %bitcast_add_fusion.2 = f32[8,16,96,96]{2,3,1,0:T(8,128)} fusion(f32[8,16,96,96]{2,3,1,0:T(8,128)} %get-tuple-element.171, pred[]{:T(512)S(6)} %compare.8, bf16[8,16,96,96]{3,2,1,0:T(8,128)(2,1)S(1)} %reshape.136, bf16[16,8,96,96]{3,2,1,0:T(8,128)(2,1)} %get-tuple-element.187, s32[]{:T(128)} %get-tuple-element.170), kind=kOutput, calls=%fused_computation.4.clone.1 | convolution fusion | flops 228851712 | bytes 13566465 | tf_op jit(solution)/shard_map/while/body/eval_jaxpr/rab,rqbc->rqac/dot_general | solution.py:65
  466.8 5.7 %gather_fusion = bf16[8,16,9216]{2,1,0:T(8,128)(2,1)S(1)} fusion(bf16[48,16,9216]{2,1,0:T(8,128)(2,1)} %get-tuple-element.186, s32[1024]{0:T(1024)S(1)} %pad_clamp_fusion.2), kind=kCustom, calls=%fused_computation.2.clone.clone.1 | custom fusion | bytes 4718624 | tf_op jit(solution)/shard_map/while/body/eval_jaxpr/gather | solution.py:53
  480.3 6.8 %bitcast_add_fusion.2 = f32[8,16,96,96]{2,3,1,0:T(8,128)} fusion(f32[8,16,96,96]{2,3,1,0:T(8,128)} %get-tuple-element.171, pred[]{:T(512)S(6)} %compare.8, bf16[8,16,96,96]{3,2,1,0:T(8,128)(2,1)S(1)} %reshape.136, bf16[16,8,96,96]{3,2,1,0:T(8,128)(2,1)} %get-tuple-element.187, s32[]{:T(128)} %get-tuple-element.170), kind=kOutput, calls=%fused_computation.4.clone.1 | convolution fusion | flops 228851712 | bytes 13566465 | tf_op jit(solution)/shard_map/while/body/eval_jaxpr/rab,rqbc->rqac/dot_general | solution.py:65
  487.2 5.7 %gather_fusion = bf16[8,16,9216]{2,1,0:T(8,128)(2,1)S(1)} fusion(bf16[48,16,9216]{2,1,0:T(8,128)(2,1)} %get-tuple-element.186, s32[1024]{0:T(1024)S(1)} %pad_clamp_fusion.2), kind=kCustom, calls=%fused_computation.2.clone.clone.1 | custom fusion | bytes 4718624 | tf_op jit(solution)/shard_map/while/body/eval_jaxpr/gather | solution.py:53
  500.8 6.8 %bitcast_add_fusion.2 = f32[8,16,96,96]{2,3,1,0:T(8,128)} fusion(f32[8,16,96,96]{2,3,1,0:T(8,128)} %get-tuple-element.171, pred[]{:T(512)S(6)} %compare.8, bf16[8,16,96,96]{3,2,1,0:T(8,128)(2,1)S(1)} %reshape.136, bf16[16,8,96,96]{3,2,1,0:T(8,128)(2,1)} %get-tuple-element.187, s32[]{:T(128)} %get-tuple-element.170), kind=kOutput, calls=%fused_computation.4.clone.1 | convolution fusion | flops 228851712 | bytes 13566465 | tf_op jit(solution)/shard_map/while/body/eval_jaxpr/rab,rqbc->rqac/dot_general | solution.py:65
  507.6 5.7 %gather_fusion = bf16[8,16,9216]{2,1,0:T(8,128)(2,1)S(1)} fusion(bf16[48,16,9216]{2,1,0:T(8,128)(2,1)} %get-tuple-element.186, s32[1024]{0:T(1024)S(1)} %pad_clamp_fusion.2), kind=kCustom, calls=%fused_computation.2.clone.clone.1 | custom fusion | bytes 4718624 | tf_op jit(solution)/shard_map/while/body/eval_jaxpr/gather | solution.py:53
  521.2 6.8 %bitcast_add_fusion.2 = f32[8,16,96,96]{2,3,1,0:T(8,128)} fusion(f32[8,16,96,96]{2,3,1,0:T(8,128)} %get-tuple-element.171, pred[]{:T(512)S(6)} %compare.8, bf16[8,16,96,96]{3,2,1,0:T(8,128)(2,1)S(1)} %reshape.136, bf16[16,8,96,96]{3,2,1,0:T(8,128)(2,1)} %get-tuple-element.187, s32[]{:T(128)} %get-tuple-element.170), kind=kOutput, calls=%fused_computation.4.clone.1 | convolution fusion | flops 228851712 | bytes 13566465 | tf_op jit(solution)/shard_map/while/body/eval_jaxpr/rab,rqbc->rqac/dot_general | solution.py:65
  534.4 6.7 %reshape.89 = bf16[2,4,16,9216]{3,2,1,0:T(8,128)(2,1)} reshape(bf16[8,16,96,96]{3,2,1,0:T(8,128)(2,1)} %copy.10) | data formatting | bytes 4718592 | tf_op jit(solution)/shard_map/reshape | solution.py:72
  (160 shorter events, 120.4 us)
Async XLA Ops:
  0.0 57.6 %copy-start.1 = (bf16[2,4,16,9216]{3,2,1,0:T(8,128)(2,1)S(1)}, bf16[2,4,16,9216]{3,2,1,0:T(8,128)(2,1)}, u32[]{:S(2)}) copy-start(bf16[2,4,16,9216]{3,2,1,0:T(8,128)(2,1)} %param.8) | copy-start | bytes 7077892
  0.0 57.5 %collective-permute-start.8 = (bf16[2,4,16,9216]{3,2,1,0:T(8,128)(2,1)}, bf16[2,4,16,9216]{3,2,1,0:T(8,128)(2,1)S(1)}, u32[]{:S(2)}, u32[]{:S(2)}) collective-permute-start(bf16[2,4,16,9216]{3,2,1,0:T(8,128)(2,1)} %param.8), channel_id=1, source_target_pairs={{0,1},{1,2},{2,3},{3,0},{4,5},{5,6},{6,7},{7,4},{8,9},{9,10},{10,1... | collective-permute-start | bytes 7077896 | tf_op jit(solution)/shard_map/ppermute | solution.py:16
  3.0 103.5 %collective-permute-start.9 = (bf16[2,4,16,9216]{3,2,1,0:T(8,128)(2,1)}, bf16[2,4,16,9216]{3,2,1,0:T(8,128)(2,1)S(1)}, u32[]{:S(2)}, u32[]{:S(2)}) collective-permute-start(bf16[2,4,16,9216]{3,2,1,0:T(8,128)(2,1)} %param.8), channel_id=1, source_target_pairs={{1,0},{2,1},{3,2},{0,3},{5,4},{6,5},{7,6},{4,7},{9,8},{10,9},{11,1... | collective-permute-start | bytes 7077896 | tf_op jit(solution)/shard_map/ppermute | solution.py:17
  106.7 5.4 copy-start
  106.7 7.1 %copy-start.3 = (s32[2,4,16]{2,1,0:T(4,128)S(1)}, s32[2,4,16]{2,1,0:T(4,128)}, u32[]{:S(2)}) copy-start(s32[2,4,16]{2,1,0:T(4,128)} %param.9) | copy-start | bytes 1540
  106.7 10.9 %copy-start.5 = (s32[2,4,16]{2,1,0:T(4,128)S(1)}, s32[2,4,16]{2,1,0:T(4,128)}, u32[]{:S(2)}) copy-start(s32[2,4,16]{2,1,0:T(4,128)} %param.11) | copy-start | bytes 1540
  106.7 10.9 %copy-start.2 = (bf16[2,4,16,9216]{3,2,1,0:T(8,128)(2,1)S(1)}, bf16[2,4,16,9216]{3,2,1,0:T(8,128)(2,1)}, u32[]{:S(2)}) copy-start(bf16[2,4,16,9216]{3,2,1,0:T(8,128)(2,1)} %param.7) | copy-start | bytes 7077892
  112.1 78.7 %collective-permute-start.10 = (bf16[6,2,16,9216]{3,2,1,0:T(8,128)(2,1)}, bf16[6,2,16,9216]{3,2,1,0:T(8,128)(2,1)}, u32[]{:S(2)}, u32[]{:S(2)}) collective-permute-start(bf16[6,2,16,9216]{3,2,1,0:T(8,128)(2,1)} %get-tuple-element.99), channel_id=1, source_target_pairs={{0,4},{4,8},{8,12},{12,0},{1,5},{5,9},{9,13},{13,1},{2,6},{6,10},{... | collective-permute-start | bytes 10616840 | tf_op jit(solution)/shard_map/ppermute | solution.py:16
  112.1 78.7 %collective-permute-start.11 = (bf16[6,2,16,9216]{3,2,1,0:T(8,128)(2,1)}, bf16[6,2,16,9216]{3,2,1,0:T(8,128)(2,1)}, u32[]{:S(2)}, u32[]{:S(2)}) collective-permute-start(bf16[6,2,16,9216]{3,2,1,0:T(8,128)(2,1)} %get-tuple-element.100), channel_id=1, source_target_pairs={{4,0},{8,4},{12,8},{0,12},{5,1},{9,5},{13,9},{1,13},{6,2},{10,6},{... | collective-permute-start | bytes 10616840 | tf_op jit(solution)/shard_map/ppermute | solution.py:17
  113.8 14.1 %collective-permute-start = (s32[2,4,16]{2,1,0:T(4,128)S(1)}, s32[2,4,16]{2,1,0:T(4,128)S(1)}, u32[]{:S(2)}, u32[]{:S(2)}) collective-permute-start(s32[2,4,16]{2,1,0:T(4,128)S(1)} %copy-done.3), channel_id=1, source_target_pairs={{0,1},{1,2},{2,3},{3,0},{4,5},{5,6},{6,7},{7,4},{8,9},{9,10},{10,1... | collective-permute-start | bytes 1544 | tf_op jit(solution)/shard_map/ppermute | solution.py:16
  115.0 16.8 %collective-permute-start.1 = (s32[2,4,16]{2,1,0:T(4,128)S(1)}, s32[2,4,16]{2,1,0:T(4,128)S(1)}, u32[]{:S(2)}, u32[]{:S(2)}) collective-permute-start(s32[2,4,16]{2,1,0:T(4,128)S(1)} %copy-done.3), channel_id=1, source_target_pairs={{1,0},{2,1},{3,2},{0,3},{5,4},{6,5},{7,6},{4,7},{9,8},{10,9},{11,1... | collective-permute-start | bytes 1544 | tf_op jit(solution)/shard_map/ppermute | solution.py:17
  117.6 14.3 %collective-permute-start.4 = (s32[2,4,16]{2,1,0:T(4,128)S(1)}, s32[2,4,16]{2,1,0:T(4,128)S(1)}, u32[]{:S(2)}, u32[]{:S(2)}) collective-permute-start(s32[2,4,16]{2,1,0:T(4,128)S(1)} %copy-done.5), channel_id=1, source_target_pairs={{0,1},{1,2},{2,3},{3,0},{4,5},{5,6},{6,7},{7,4},{8,9},{9,10},{10,1... | collective-permute-start | bytes 1544 | tf_op jit(solution)/shard_map/ppermute | solution.py:16
  120.9 4.9 copy-start.4
  127.9 5.8 %collective-permute-start.5 = (s32[2,4,16]{2,1,0:T(4,128)S(1)}, s32[2,4,16]{2,1,0:T(4,128)S(1)}, u32[]{:S(2)}, u32[]{:S(2)}) collective-permute-start(s32[2,4,16]{2,1,0:T(4,128)S(1)} %copy-done.5), channel_id=1, source_target_pairs={{1,0},{2,1},{3,2},{0,3},{5,4},{6,5},{7,6},{4,7},{9,8},{10,9},{11,1... | collective-permute-start | bytes 1544 | tf_op jit(solution)/shard_map/ppermute | solution.py:17
  131.8 57.5 %collective-permute-start.2 = (s32[6,2,16]{2,1,0:T(2,128)S(1)}, s32[6,2,16]{2,1,0:T(2,128)S(1)}, u32[]{:S(2)}, u32[]{:S(2)}) collective-permute-start(s32[6,2,16]{2,1,0:T(2,128)S(1)} %get-tuple-element.103), channel_id=1, source_target_pairs={{0,4},{4,8},{8,12},{12,0},{1,5},{5,9},{9,13},{13,1},{2,6},{6,10},{... | collective-permute-start | bytes 2312 | tf_op jit(solution)/shard_map/ppermute | solution.py:16
  131.9 58.5 %collective-permute-start.3 = (s32[6,2,16]{2,1,0:T(2,128)S(1)}, s32[6,2,16]{2,1,0:T(2,128)S(1)}, u32[]{:S(2)}, u32[]{:S(2)}) collective-permute-start(s32[6,2,16]{2,1,0:T(2,128)S(1)} %get-tuple-element.104), channel_id=1, source_target_pairs={{4,0},{8,4},{12,8},{0,12},{5,1},{9,5},{13,9},{1,13},{6,2},{10,6},{... | collective-permute-start | bytes 2312 | tf_op jit(solution)/shard_map/ppermute | solution.py:17
  133.7 56.7 %collective-permute-start.6 = (s32[6,2,16]{2,1,0:T(2,128)S(1)}, s32[6,2,16]{2,1,0:T(2,128)S(1)}, u32[]{:S(2)}, u32[]{:S(2)}) collective-permute-start(s32[6,2,16]{2,1,0:T(2,128)S(1)} %get-tuple-element.101), channel_id=1, source_target_pairs={{0,4},{4,8},{8,12},{12,0},{1,5},{5,9},{9,13},{13,1},{2,6},{6,10},{... | collective-permute-start | bytes 2312 | tf_op jit(solution)/shard_map/ppermute | solution.py:16
  189.3 1.4 collective-permute-start.7
where the time goes:
time: 546 us; the launch traced here: 541 us
  local copies, waits for them, and re-layouts  204 us (37%)
  waiting for transfers between devices  158 us (29%)
  matrix products  143 us (26%)
  other arithmetic  18.3 us (3%)
  starting transfers between devices  16.3 us (3%)
    ppermute x6, waiting for transfers between devices, padded(): before = lax.ppermute(last, axis, up)  108 us
    dot_general x16, matrix products, add_group(): jnp.einsum('rab,rqbc->rqac', left_group, picked, preferred_element_type=j...  108 us
    gather x16, local copies, waits for them, and re-layouts, add_group(): source_tiles = flat_tiles[rows_at]  91.5 us
    reshape x16, local copies, waits for them, and re-layouts, add_group(): picked = picked.reshape(rows_here, slot_count, BS, BS)  71.5 us
    ppermute x6, waiting for transfers between devices, padded(): after = lax.ppermute(initial, axis, down)  50 us
    dot_general x16, matrix products, add_group(): jnp.einsum('rqs,rsn->rqn', select, source_tiles, preferred_element_type=j...  35.6 us
    concatenate x1, other arithmetic, padded(): array = jnp.concatenate([before, array, after], axis=dim)  12.4 us
    ppermute x6, starting transfers between devices, padded(): after = lax.ppermute(initial, axis, down)  12 us
  transfers between devices with their start and end apart: 12, of which 5 were waited for; matrix products, arithmetic and copies ran while one was open for 2% of the time, Pallas kernels for 0%

commit v1 on v0

v1 whole, which is shorter than its diff:
```python
import functools

import jax
import jax.numpy as jnp
from jax import lax
from jax.experimental import pallas as pl
from jax.experimental.pallas import tpu as pltpu
from jax.sharding import PartitionSpec as P

BS = 96
LANES = 128
REACH = 2
GROUP = 2


def shift(array, axis, step):
    peers = lax.axis_size(axis)
    return lax.ppermute(array, axis, [(i, (i + step) % peers) for i in range(peers)])


def halo(low, high):
    own = (low, high)
    before_x = [shift(p, "col", 1) for p in own]
    after_x = [shift(p, "col", -1) for p in own]
    rows = []
    for mid in (before_x, own, after_x):
        rows.append([shift(mid[1], "row", 1), mid[0], mid[1], shift(mid[0], "row", -1)])
    return rows


def product_kernel(slots, pieces, *refs):
    table = refs[0]
    left = refs[1]
    sources = refs[2 : 2 + pieces]
    out = refs[2 + pieces]
    near, wide_a, wide_b, sems = refs[3 + pieces :]
    span = near.shape[0] // pieces
    copies = [
        pltpu.make_async_copy(src, near.at[pl.ds(n * span, span)], sems.at[n])
        for n, src in enumerate(sources)
    ]
    for copy in copies:
        copy.start()
    for copy in copies:
        copy.wait()
    buffers = (wide_a, wide_b)
    rows = left.shape[0]

    def gather(row, first, wide):
        for g in range(slots):
            for u in range(GROUP):
                at = table[(row * slots + g) * slots + first + u]
                tile = near[jnp.maximum(at, 0)]
                tile = jnp.where(at >= 0, tile, jnp.zeros_like(tile))
                wide[g * BS : (g + 1) * BS, u * LANES : u * LANES + BS] = tile

    def one_row(row, carry):
        lhs = left[row]
        turns = slots // GROUP
        for turn in range(turns):
            wide = buffers[turn % 2]
            gather(row, turn * GROUP, wide)
            total = jnp.dot(lhs, wide[...], preferred_element_type=jnp.float32)
            total = (0.5 * total).astype(out.dtype)
            for u in range(GROUP):
                out[row, turn * GROUP + u] = total[:, u * LANES : u * LANES + BS]
        return carry

    lax.fori_loop(0, rows, one_row, 0)


def body(left_blocks, right_blocks, pattern, left_live, right_live):
    cells_x, cells_y, slots, area = left_blocks.shape
    rows = cells_x * cells_y
    assert cells_x == REACH and cells_y == 2 * REACH
    grid_x = cells_x * lax.axis_size("col")
    grid_y = cells_y * lax.axis_size("row")

    codes = pattern * 2 + (right_live != 0).astype(jnp.int32)
    code_pieces = halo(codes[:, :REACH], codes[:, REACH:])
    tile_pieces = halo(right_blocks[:, :REACH], right_blocks[:, REACH:])
    cells = REACH * REACH
    near_codes = jnp.concatenate(
        [p.reshape(cells, slots) for line in code_pieces for p in line], axis=0
    )
    sources = [
        p.reshape(cells * slots, BS, BS) for line in tile_pieces for p in line
    ]

    local_x = jnp.arange(cells_x, dtype=jnp.int32)[:, None, None]
    local_y = jnp.arange(cells_y, dtype=jnp.int32)[None, :, None]
    own_x = lax.axis_index("col") * cells_x + local_x
    own_y = lax.axis_index("row") * cells_y + local_y
    near_x = local_x + (pattern // grid_y - own_x + REACH) % grid_x
    near_y = local_y + (pattern % grid_y - own_y + REACH) % grid_y
    piece = (near_x // REACH) * 4 + near_y // REACH
    place = piece * cells + (near_x % REACH) * REACH + near_y % REACH
    place = place.reshape(rows, slots)
    targets = pattern.reshape(rows, slots)
    picked = near_codes[place]
    live = (picked % 2 == 1) & (left_live.reshape(rows, slots) != 0)[:, :, None]
    match = (picked[:, :, None, :] // 2 == targets[:, None, :, None]) & live[:, :, None, :]
    found = jnp.where(match, jnp.arange(slots, dtype=jnp.int32) + 1, 0).max(axis=3)
    table = jnp.where(found > 0, place[:, :, None] * slots + found - 1, -1).reshape(-1)

    left = left_blocks.reshape(rows, slots, BS, BS)
    left = jnp.moveaxis(left, 1, 2).reshape(rows, BS, slots * BS)

    count = len(sources)
    vmem = pl.BlockSpec(memory_space=pltpu.VMEM)
    out = pl.pallas_call(
        functools.partial(product_kernel, slots, count),
        out_shape=jax.ShapeDtypeStruct((rows, slots, BS, BS), jnp.bfloat16),
        in_specs=[pl.BlockSpec(memory_space=pltpu.SMEM), vmem]
        + [pl.BlockSpec(memory_space=pl.ANY)] * count,
        out_specs=vmem,
        scratch_shapes=[
            pltpu.VMEM((count * cells * slots, BS, BS), jnp.bfloat16),
            pltpu.VMEM((slots * BS, GROUP * LANES), jnp.bfloat16),
            pltpu.VMEM((slots * BS, GROUP * LANES), jnp.bfloat16),
            pltpu.SemaphoreType.DMA((count,)),
        ],
        compiler_params=pltpu.CompilerParams(vmem_limit_bytes=36 * 1024 * 1024),
        cost_estimate=pl.CostEstimate(
            flops=2 * rows * slots * slots * BS**3,
            bytes_accessed=2 * (count * cells + 2 * rows) * slots * area,
            transcendentals=0,
        ),
    )(table, left, *sources)
    return out.reshape(cells_x, cells_y, slots, area)


def solution(mesh):
    placed = (
        P(("win", "col"), "row", None, None),
        P(("win", "col"), "row", None, None),
        P(("win", "col"), "row", None),
        P(("win", "col"), "row", None),
        P(("win", "col"), "row", None),
    )
    return jax.shard_map(
        body,
        mesh=mesh,
        in_specs=placed,
        out_specs=P(("win", "col"), "row", None, None),
        check_vma=False,
    )
```

time: 546 us -> 226 us (0.41)
  matrix products: 143 us -> 0 us
  local copies, waits for them, and re-layouts: 204 us -> 80.2 us
  waiting for transfers between devices: 158 us -> 93.8 us
  Pallas kernels: 0 us -> 26.9 us
  other arithmetic: 18.3 us -> 3.35 us
    dot_general x32 -> x0, matrix products: 143 us -> none  [the longest x16 108 us: add_group(): jnp.einsum('rab,rqbc->rqac', left_group, picked, preferred_element_type=j...]
    gather x48 -> x1, local copies, waits for them, and re-layouts: 109 us -> 0.64 us  [body(): picked = near_codes[place]]
    ppermute x12 -> x20, waiting for transfers between devices: 158 us -> 93.8 us  [shift(): lax.ppermute(array, axis, [(i, (i + step) % peers) for i in range(peers)])]
    pallas_call x0 -> x1, Pallas kernels: none -> 26.9 us  [body(): pl.pallas_call(functools.partial(product_kernel, slots, count), out_shape...]
    reshape x18 -> x16, local copies, waits for them, and re-layouts: 83.1 us -> 63.7 us  [the longest x12 40.2 us: body(): p.reshape(cells * slots, BS, BS)]
    concatenate x1 -> x0, other arithmetic: 12.4 us -> none  [padded(): array = jnp.concatenate([before, array, after], axis=dim)]
    unnamed x19 -> x26, local copies, waits for them, and re-layouts: 5.68 us -> 12.7 us
    ppermute x12 -> x20, starting transfers between devices: 16.3 us -> 20.3 us  [shift(): lax.ppermute(array, axis, [(i, (i + step) % peers) for i in range(peers)])]
  transfers between devices with their start and end apart: 12 -> 20, of which waited for: 5 -> 4; matrix products, arithmetic and copies ran while one was open for 2% -> 27% of each run, Pallas kernels for 0% -> 0%
where the time goes in v1:
time: 226 us; the launch traced here: 225 us
  waiting for transfers between devices  93.8 us (42%)
  local copies, waits for them, and re-layouts  80.2 us (35%)
  Pallas kernels  26.9 us (12%)
  starting transfers between devices  20.3 us (9%)
  other arithmetic  3.35 us (1%)
    ppermute x20, waiting for transfers between devices, shift(): lax.ppermute(array, axis, [(i, (i + step) % peers) for i in range(peers)])  93.8 us
    reshape x12, local copies, waits for them, and re-layouts, body(): p.reshape(cells * slots, BS, BS)  40.2 us
    pallas_call x1, Pallas kernels, body(): pl.pallas_call(functools.partial(product_kernel, slots, count), out_shape...  26.9 us
    ppermute x20, starting transfers between devices, shift(): lax.ppermute(array, axis, [(i, (i + step) % peers) for i in range(peers)])  20.3 us
    unnamed x26, local copies, waits for them, and re-layouts  12.7 us
    reshape x2, local copies, waits for them, and re-layouts, body(): left = left_blocks.reshape(rows, slots, BS, BS)  10.4 us
    reshape x1, local copies, waits for them, and re-layouts, body(): return out.reshape(cells_x, cells_y, slots, area)  6.69 us
    reshape x1, local copies, waits for them, and re-layouts, body(): left = jnp.moveaxis(left, 1, 2).reshape(rows, BS, slots * BS)  6.41 us
  transfers between devices with their start and end apart: 20, of which 4 were waited for; matrix products, arithmetic and copies ran while one was open for 27% of the time, Pallas kernels for 0%

profile of v1, /device:TPU:0, one launch (start us, length us, event | category | flops | bytes accessed | tf_op | source)
XLA Modules:
  0.0 224.7 jit_solution(1381512305439376202)
XLA Ops:
  0.0 0.8 broadcast_multiply_fusion
  0.8 3.1 %collective-permute-start = (s32[2,2,16]{2,1,0:T(2,128)S(1)}, s32[2,2,16]{2,1,0:T(2,128)S(1)}, u32[]{:S(2)}, u32[]{:S(2)}) collective-permute-start(s32[2,2,16]{2,1,0:T(2,128)S(1)} %get-tuple-element.11), channel_id=1, source_target_pairs={{0,1},{1,2},{2,3},{3,0},{4,5},{5,6},{6,7},{7,4},{8,9},{9,10},{10,1... | collective-permute-start | bytes 776 | tf_op jit(solution)/shard_map/ppermute | solution.py:18
  3.9 1.6 collective-permute-start.2
  5.5 1.5 collective-permute-start.5
  7.0 2.2 %collective-permute-start.6 = (s32[2,2,16]{2,1,0:T(2,128)S(1)}, s32[2,2,16]{2,1,0:T(2,128)S(1)}, u32[]{:S(2)}, u32[]{:S(2)}) collective-permute-start(s32[2,2,16]{2,1,0:T(2,128)S(1)} %get-tuple-element.11), channel_id=1, source_target_pairs={{0,3},{1,0},{2,1},{3,2},{4,7},{5,4},{6,5},{7,6},{8,11},{9,8},{10,9... | collective-permute-start | bytes 776 | tf_op jit(solution)/shard_map/ppermute | solution.py:18
  9.2 2.9 %fusion.24 = (bf16[2,2,16,9216]{3,2,1,0:T(8,128)(2,1)}, bf16[2,2,16,9216]{3,2,1,0:T(8,128)(2,1)S(1)}) fusion(bf16[2,4,16,9216]{3,2,1,0:T(8,128)(2,1)} %param.6), kind=kLoop, calls=%fused_computation.65 | loop fusion | bytes 4718592 | tf_op jit(solution)/shard_map/slice | solution.py:81
  12.1 0.5 collective-permute-start.8
  12.6 1.5 collective-permute-start.10
  14.1 1.7 collective-permute-start.3
  15.9 1.7 collective-permute-start.9
  17.7 1.5 collective-permute-start.14
  19.2 2.3 %collective-permute-start.16 = (bf16[2,2,16,9216]{3,2,1,0:T(8,128)(2,1)S(1)}, bf16[2,2,16,9216]{3,2,1,0:T(8,128)(2,1)}, u32[]{:S(2)}, u32[]{:S(2)}) collective-permute-start(bf16[2,2,16,9216]{3,2,1,0:T(8,128)(2,1)S(1)} %get-tuple-element.8), channel_id=1, source_target_pairs={{0,3},{1,0},{2,1},{3,2},{4,7},{5,4},{6,5},{7,6},{8,11},{9,8},{10,9... | collective-permute-start | bytes 3538952 | tf_op jit(solution)/shard_map/ppermute | solution.py:18
  21.5 0.5 collective-permute-start.18
  22.0 21.5 %collective-permute-done.10 = bf16[2,2,16,9216]{3,2,1,0:T(8,128)(2,1)} collective-permute-done((bf16[2,2,16,9216]{3,2,1,0:T(8,128)(2,1)S(1)}, bf16[2,2,16,9216]{3,2,1,0:T(8,128)(2,1)}, u32[]{:S(2)}, u32[]{:S(2)}) %collective-permute-start.10) | collective-permute-done | bytes 1179680 | tf_op jit(solution)/shard_map/ppermute | solution.py:18
  43.6 25.2 %collective-permute-done.12 = bf16[2,2,16,9216]{3,2,1,0:T(8,128)(2,1)} collective-permute-done((bf16[2,2,16,9216]{3,2,1,0:T(8,128)(2,1)}, bf16[2,2,16,9216]{3,2,1,0:T(8,128)(2,1)}, u32[]{:S(2)}, u32[]{:S(2)}) %collective-permute-start.12) | collective-permute-done | bytes 1179680 | tf_op jit(solution)/shard_map/ppermute | solution.py:18
  68.7 1.7 collective-permute-start.13
  70.5 21.9 %collective-permute-done.16 = bf16[2,2,16,9216]{3,2,1,0:T(8,128)(2,1)} collective-permute-done((bf16[2,2,16,9216]{3,2,1,0:T(8,128)(2,1)S(1)}, bf16[2,2,16,9216]{3,2,1,0:T(8,128)(2,1)}, u32[]{:S(2)}, u32[]{:S(2)}) %collective-permute-start.16) | collective-permute-done | bytes 1179680 | tf_op jit(solution)/shard_map/ppermute | solution.py:18
  92.3 25.2 %collective-permute-done.18 = bf16[2,2,16,9216]{3,2,1,0:T(8,128)(2,1)} collective-permute-done((bf16[2,2,16,9216]{3,2,1,0:T(8,128)(2,1)}, bf16[2,2,16,9216]{3,2,1,0:T(8,128)(2,1)}, u32[]{:S(2)}, u32[]{:S(2)}) %collective-permute-start.18) | collective-permute-done | bytes 1179680 | tf_op jit(solution)/shard_map/ppermute | solution.py:18
  117.5 0.3 collective-permute-start.19
  117.8 2.6 %reshape.220.refs_7_ = bf16[64,96,96]{2,1,0:T(8,128)(2,1)S(1)} reshape(bf16[2,2,16,9216]{3,2,1,0:T(8,128)(2,1)} %get-tuple-element.7) | data formatting | bytes 2359296 | tf_op jit(solution)/shard_map/reshape | solution.py:87
  120.4 2.6 %reshape.221.refs_8_ = bf16[64,96,96]{2,1,0:T(8,128)(2,1)S(1)} reshape(bf16[2,2,16,9216]{3,2,1,0:T(8,128)(2,1)} %copy-done.9) | data formatting | bytes 2359296 | tf_op jit(solution)/shard_map/reshape | solution.py:87
  123.1 5.6 %reshape.213 = bf16[8,16,96,96]{3,2,1,0:T(8,128)(2,1)} reshape(bf16[2,4,16,9216]{3,2,1,0:T(8,128)(2,1)} %param.5) | data formatting | bytes 4718592 | tf_op jit(solution)/shard_map/reshape | solution.py:106
  128.8 4.8 %copy.23 = bf16[8,16,96,96]{3,1,2,0:T(8,128)(2,1)} copy(bf16[8,16,96,96]{3,2,1,0:T(8,128)(2,1)} %reshape.213) | data formatting | bytes 4718592 | tf_op jit(solution)/shard_map/reshape | solution.py:106
  133.6 6.4 %reshape.214.refs_1_ = bf16[8,96,1536]{2,1,0:T(8,128)(2,1)} reshape(bf16[8,96,16,96]{3,2,1,0:T(8,128)(2,1)} %bitcast.52) | data formatting | bytes 4718592 | tf_op jit(solution)/shard_map/reshape | solution.py:107
  140.0 0.1 concatenate.3
  140.1 0.6 gather_fusion
  140.9 2.3 %select_reduce_fusion = s32[8,16,16]{2,1,0:T(8,128)S(1)} fusion(s32[16]{0:T(128)S(1)} %iota_add_fusion, s32[8,16]{1,0:T(8,128)S(1)} %bitcast.55, s32[8,16,16]{2,1,0:T(8,128)S(1)} %add_select_fusion.1, pred[8,16,16]{2,1,0:T(8,128)(4,1)S(1)} %fusion.2), kind=kLoop, calls=%fused_computation.2 | loop fusion | flops 129024 | bytes 19008 | tf_op jit(solution)/shard_map/reduce_max | solution.py:103
  143.4 3.5 %reshape.216.refs_3_ = bf16[64,96,96]{2,1,0:T(8,128)(2,1)} reshape(bf16[2,2,16,9216]{3,2,1,0:T(8,128)(2,1)} %collective-permute-done.12) | data formatting | bytes 2359296 | tf_op jit(solution)/shard_map/reshape | solution.py:87
  147.0 3.5 %reshape.217.refs_4_ = bf16[64,96,96]{2,1,0:T(8,128)(2,1)} reshape(bf16[2,2,16,9216]{3,2,1,0:T(8,128)(2,1)} %collective-permute-done.10) | data formatting | bytes 2359296 | tf_op jit(solution)/shard_map/reshape | solution.py:87
  150.4 3.5 %reshape.224.refs_11_ = bf16[64,96,96]{2,1,0:T(8,128)(2,1)} reshape(bf16[2,2,16,9216]{3,2,1,0:T(8,128)(2,1)} %collective-permute-done.18) | data formatting | bytes 2359296 | tf_op jit(solution)/shard_map/reshape | solution.py:87
  153.9 3.5 %reshape.225.refs_12_ = bf16[64,96,96]{2,1,0:T(8,128)(2,1)} reshape(bf16[2,2,16,9216]{3,2,1,0:T(8,128)(2,1)} %collective-permute-done.16) | data formatting | bytes 2359296 | tf_op jit(solution)/shard_map/reshape | solution.py:87
  157.4 3.5 %reshape.219.refs_6_ = bf16[64,96,96]{2,1,0:T(8,128)(2,1)} reshape(bf16[2,2,16,9216]{3,2,1,0:T(8,128)(2,1)} %copy-done.10) | data formatting | bytes 2359296 | tf_op jit(solution)/shard_map/reshape | solution.py:87
  160.9 3.5 %reshape.222.refs_9_ = bf16[64,96,96]{2,1,0:T(8,128)(2,1)} reshape(bf16[2,2,16,9216]{3,2,1,0:T(8,128)(2,1)} %collective-permute-done.15) | data formatting | bytes 2359296 | tf_op jit(solution)/shard_map/reshape | solution.py:87
  164.4 3.5 %reshape.215.refs_2_ = bf16[64,96,96]{2,1,0:T(8,128)(2,1)} reshape(bf16[2,2,16,9216]{3,2,1,0:T(8,128)(2,1)} %collective-permute-done.11) | data formatting | bytes 2359296 | tf_op jit(solution)/shard_map/reshape | solution.py:87
  167.9 3.5 %reshape.218.refs_5_ = bf16[64,96,96]{2,1,0:T(8,128)(2,1)} reshape(bf16[2,2,16,9216]{3,2,1,0:T(8,128)(2,1)} %collective-permute-done.13) | data formatting | bytes 2359296 | tf_op jit(solution)/shard_map/reshape | solution.py:87
  171.4 3.5 %reshape.223.refs_10_ = bf16[64,96,96]{2,1,0:T(8,128)(2,1)} reshape(bf16[2,2,16,9216]{3,2,1,0:T(8,128)(2,1)} %collective-permute-done.17) | data formatting | bytes 2359296 | tf_op jit(solution)/shard_map/reshape | solution.py:87
  174.9 3.5 %reshape.226.refs_13_ = bf16[64,96,96]{2,1,0:T(8,128)(2,1)} reshape(bf16[2,2,16,9216]{3,2,1,0:T(8,128)(2,1)} %collective-permute-done.19) | data formatting | bytes 2359296 | tf_op jit(solution)/shard_map/reshape | solution.py:87
  178.4 1.4 copy-done
  179.8 1.4 copy-done.1
  181.2 1.4 copy-done.2
  182.7 1.4 copy-done.3
  184.1 1.4 copy-done.4
  185.5 1.4 copy-done.5
  186.9 1.4 copy-done.6
  188.3 1.4 copy-done.7
  189.7 1.4 copy-done.8
  191.1 26.9 %shard_map.55 = bf16[8,16,96,96]{3,2,1,0:T(8,128)(2,1)} custom-call(s32[2048]{0:T(1024)S(1)} %select_n.89.refs_0_, bf16[8,96,1536]{2,1,0:T(8,128)(2,1)} %reshape.214.refs_1_, bf16[64,96,96]{2,1,0:T(8,128)(2,1)S(1)} %copy-done.6, bf16[64,96,96]{2,1,0:T(8,128)(2,1)S(1)} %copy-done, bf16[64,96,96]{2,1,0:T(8,128)(2,1)S(1)} %copy-done.1, ...), custom_call_target="tpu_custom_call" | custom-call | flops 3623878656 | bytes 18874368 | tf_op jit(solution)/shard_map/pallas_call | solution.py:111
  218.0 6.7 %reshape.227 = bf16[2,4,16,9216]{3,2,1,0:T(8,128)(2,1)} reshape(bf16[8,16,96,96]{3,2,1,0:T(8,128)(2,1)} %shard_map.55) | data formatting | bytes 4718592 | tf_op jit(solution)/shard_map/reshape | solution.py:130
  (52 shorter events, 0.5 us)
Async XLA Ops:
  0.8 11.3 %collective-permute-start = (s32[2,2,16]{2,1,0:T(2,128)S(1)}, s32[2,2,16]{2,1,0:T(2,128)S(1)}, u32[]{:S(2)}, u32[]{:S(2)}) collective-permute-start(s32[2,2,16]{2,1,0:T(2,128)S(1)} %get-tuple-element.11), channel_id=1, source_target_pairs={{0,1},{1,2},{2,3},{3,0},{4,5},{5,6},{6,7},{7,4},{8,9},{9,10},{10,1... | collective-permute-start | bytes 776 | tf_op jit(solution)/shard_map/ppermute | solution.py:18
  3.9 10.2 %collective-permute-start.4 = (s32[2,2,16]{2,1,0:T(2,128)S(1)}, s32[2,2,16]{2,1,0:T(2,128)S(1)}, u32[]{:S(2)}, u32[]{:S(2)}) collective-permute-start(s32[2,2,16]{2,1,0:T(2,128)S(1)} %get-tuple-element.11), channel_id=1, source_target_pairs={{0,4},{4,8},{8,12},{12,0},{1,5},{5,9},{9,13},{13,1},{2,6},{6,10},{... | collective-permute-start | bytes 776 | tf_op jit(solution)/shard_map/ppermute | solution.py:18
  3.9 8.7 %collective-permute-start.2 = (s32[2,2,16]{2,1,0:T(2,128)S(1)}, s32[2,2,16]{2,1,0:T(2,128)S(1)}, u32[]{:S(2)}, u32[]{:S(2)}) collective-permute-start(s32[2,2,16]{2,1,0:T(2,128)S(1)} %get-tuple-element.10), channel_id=1, source_target_pairs={{0,1},{1,2},{2,3},{3,0},{4,5},{5,6},{6,7},{7,4},{8,9},{9,10},{10,1... | collective-permute-start | bytes 776 | tf_op jit(solution)/shard_map/ppermute | solution.py:18
  5.5 8.6 %collective-permute-start.5 = (s32[2,2,16]{2,1,0:T(2,128)S(1)}, s32[2,2,16]{2,1,0:T(2,128)S(1)}, u32[]{:S(2)}, u32[]{:S(2)}) collective-permute-start(s32[2,2,16]{2,1,0:T(2,128)S(1)} %get-tuple-element.10), channel_id=1, source_target_pairs={{0,12},{4,0},{8,4},{12,8},{1,13},{5,1},{9,5},{13,9},{2,14},{6,2},{... | collective-permute-start | bytes 776 | tf_op jit(solution)/shard_map/ppermute | solution.py:18
  7.0 8.9 %collective-permute-start.6 = (s32[2,2,16]{2,1,0:T(2,128)S(1)}, s32[2,2,16]{2,1,0:T(2,128)S(1)}, u32[]{:S(2)}, u32[]{:S(2)}) collective-permute-start(s32[2,2,16]{2,1,0:T(2,128)S(1)} %get-tuple-element.11), channel_id=1, source_target_pairs={{0,3},{1,0},{2,1},{3,2},{4,7},{5,4},{6,5},{7,6},{8,11},{9,8},{10,9... | collective-permute-start | bytes 776 | tf_op jit(solution)/shard_map/ppermute | solution.py:18
  12.1 105.7 %copy-start.9 = (bf16[2,2,16,9216]{3,2,1,0:T(8,128)(2,1)}, bf16[2,2,16,9216]{3,2,1,0:T(8,128)(2,1)S(1)}, u32[]{:S(2)}) copy-start(bf16[2,2,16,9216]{3,2,1,0:T(8,128)(2,1)S(1)} %get-tuple-element.8) | copy-start | bytes 3538948
  12.1 3.8 %collective-permute-start.8 = (s32[2,2,16]{2,1,0:T(2,128)S(1)}, s32[2,2,16]{2,1,0:T(2,128)S(1)}, u32[]{:S(2)}, u32[]{:S(2)}) collective-permute-start(s32[2,2,16]{2,1,0:T(2,128)S(1)} %get-tuple-element.10), channel_id=1, source_target_pairs={{0,3},{1,0},{2,1},{3,2},{4,7},{5,4},{6,5},{7,6},{8,11},{9,8},{10,9... | collective-permute-start | bytes 776 | tf_op jit(solution)/shard_map/ppermute | solution.py:18
  12.6 31.0 %collective-permute-start.10 = (bf16[2,2,16,9216]{3,2,1,0:T(8,128)(2,1)S(1)}, bf16[2,2,16,9216]{3,2,1,0:T(8,128)(2,1)}, u32[]{:S(2)}, u32[]{:S(2)}) collective-permute-start(bf16[2,2,16,9216]{3,2,1,0:T(8,128)(2,1)S(1)} %get-tuple-element.8), channel_id=1, source_target_pairs={{0,1},{1,2},{2,3},{3,0},{4,5},{5,6},{6,7},{7,4},{8,9},{9,10},{10,1... | collective-permute-start | bytes 3538952 | tf_op jit(solution)/shard_map/ppermute | solution.py:18
  14.1 3.5 %collective-permute-start.1 = (s32[2,2,16]{2,1,0:T(2,128)S(1)}, s32[2,2,16]{2,1,0:T(2,128)S(1)}, u32[]{:S(2)}, u32[]{:S(2)}) collective-permute-start(s32[2,2,16]{2,1,0:T(2,128)S(1)} %collective-permute-done), channel_id=1, source_target_pairs={{0,4},{4,8},{8,12},{12,0},{1,5},{5,9},{9,13},{13,1},{2,6},{6,10},{... | collective-permute-start | bytes 776 | tf_op jit(solution)/shard_map/ppermute | solution.py:18
  14.1 3.6 %collective-permute-start.3 = (s32[2,2,16]{2,1,0:T(2,128)S(1)}, s32[2,2,16]{2,1,0:T(2,128)S(1)}, u32[]{:S(2)}, u32[]{:S(2)}) collective-permute-start(s32[2,2,16]{2,1,0:T(2,128)S(1)} %collective-permute-done.2), channel_id=1, source_target_pairs={{0,12},{4,0},{8,4},{12,8},{1,13},{5,1},{9,5},{13,9},{2,14},{6,2},{... | collective-permute-start | bytes 776 | tf_op jit(solution)/shard_map/ppermute | solution.py:18
  15.9 3.3 %collective-permute-start.7 = (s32[2,2,16]{2,1,0:T(2,128)S(1)}, s32[2,2,16]{2,1,0:T(2,128)S(1)}, u32[]{:S(2)}, u32[]{:S(2)}) collective-permute-start(s32[2,2,16]{2,1,0:T(2,128)S(1)} %collective-permute-done.6), channel_id=1, source_target_pairs={{0,4},{4,8},{8,12},{12,0},{1,5},{5,9},{9,13},{13,1},{2,6},{6,10},{... | collective-permute-start | bytes 776 | tf_op jit(solution)/shard_map/ppermute | solution.py:18
  15.9 5.6 %collective-permute-start.9 = (s32[2,2,16]{2,1,0:T(2,128)S(1)}, s32[2,2,16]{2,1,0:T(2,128)S(1)}, u32[]{:S(2)}, u32[]{:S(2)}) collective-permute-start(s32[2,2,16]{2,1,0:T(2,128)S(1)} %collective-permute-done.8), channel_id=1, source_target_pairs={{0,12},{4,0},{8,4},{12,8},{1,13},{5,1},{9,5},{13,9},{2,14},{6,2},{... | collective-permute-start | bytes 776 | tf_op jit(solution)/shard_map/ppermute | solution.py:18
  17.6 51.1 %collective-permute-start.12 = (bf16[2,2,16,9216]{3,2,1,0:T(8,128)(2,1)}, bf16[2,2,16,9216]{3,2,1,0:T(8,128)(2,1)}, u32[]{:S(2)}, u32[]{:S(2)}) collective-permute-start(bf16[2,2,16,9216]{3,2,1,0:T(8,128)(2,1)} %get-tuple-element.7), channel_id=1, source_target_pairs={{0,1},{1,2},{2,3},{3,0},{4,5},{5,6},{6,7},{7,4},{8,9},{9,10},{10,1... | collective-permute-start | bytes 3538952 | tf_op jit(solution)/shard_map/ppermute | solution.py:18
  17.7 51.1 %collective-permute-start.14 = (bf16[2,2,16,9216]{3,2,1,0:T(8,128)(2,1)S(1)}, bf16[2,2,16,9216]{3,2,1,0:T(8,128)(2,1)S(1)}, u32[]{:S(2)}, u32[]{:S(2)}) collective-permute-start(bf16[2,2,16,9216]{3,2,1,0:T(8,128)(2,1)S(1)} %get-tuple-element.8), channel_id=1, source_target_pairs={{0,4},{4,8},{8,12},{12,0},{1,5},{5,9},{9,13},{13,1},{2,6},{6,10},{... | collective-permute-start | bytes 3538952 | tf_op jit(solution)/shard_map/ppermute | solution.py:18
  19.2 73.2 %collective-permute-start.16 = (bf16[2,2,16,9216]{3,2,1,0:T(8,128)(2,1)S(1)}, bf16[2,2,16,9216]{3,2,1,0:T(8,128)(2,1)}, u32[]{:S(2)}, u32[]{:S(2)}) collective-permute-start(bf16[2,2,16,9216]{3,2,1,0:T(8,128)(2,1)S(1)} %get-tuple-element.8), channel_id=1, source_target_pairs={{0,3},{1,0},{2,1},{3,2},{4,7},{5,4},{6,5},{7,6},{8,11},{9,8},{10,9... | collective-permute-start | bytes 3538952 | tf_op jit(solution)/shard_map/ppermute | solution.py:18
  21.5 96.0 %collective-permute-start.18 = (bf16[2,2,16,9216]{3,2,1,0:T(8,128)(2,1)}, bf16[2,2,16,9216]{3,2,1,0:T(8,128)(2,1)}, u32[]{:S(2)}, u32[]{:S(2)}) collective-permute-start(bf16[2,2,16,9216]{3,2,1,0:T(8,128)(2,1)} %get-tuple-element.7), channel_id=1, source_target_pairs={{0,3},{1,0},{2,1},{3,2},{4,7},{5,4},{6,5},{7,6},{8,11},{9,8},{10,9... | collective-permute-start | bytes 3538952 | tf_op jit(solution)/shard_map/ppermute | solution.py:18
  43.6 117.4 %collective-permute-start.15 = (bf16[2,2,16,9216]{3,2,1,0:T(8,128)(2,1)}, bf16[2,2,16,9216]{3,2,1,0:T(8,128)(2,1)}, u32[]{:S(2)}, u32[]{:S(2)}) collective-permute-start(bf16[2,2,16,9216]{3,2,1,0:T(8,128)(2,1)} %get-tuple-element.7), channel_id=1, source_target_pairs={{0,12},{4,0},{8,4},{12,8},{1,13},{5,1},{9,5},{13,9},{2,14},{6,2},{... | collective-permute-start | bytes 3538952 | tf_op jit(solution)/shard_map/ppermute | solution.py:18
  68.7 95.7 %collective-permute-start.11 = (bf16[2,2,16,9216]{3,2,1,0:T(8,128)(2,1)}, bf16[2,2,16,9216]{3,2,1,0:T(8,128)(2,1)}, u32[]{:S(2)}, u32[]{:S(2)}) collective-permute-start(bf16[2,2,16,9216]{3,2,1,0:T(8,128)(2,1)} %collective-permute-done.10), channel_id=1, source_target_pairs={{0,4},{4,8},{8,12},{12,0},{1,5},{5,9},{9,13},{13,1},{2,6},{6,10},{... | collective-permute-start | bytes 3538952 | tf_op jit(solution)/shard_map/ppermute | solution.py:18
  68.7 49.1 %copy-start.10 = (bf16[2,2,16,9216]{3,2,1,0:T(8,128)(2,1)}, bf16[2,2,16,9216]{3,2,1,0:T(8,128)(2,1)S(1)}, u32[]{:S(2)}) copy-start(bf16[2,2,16,9216]{3,2,1,0:T(8,128)(2,1)S(1)} %collective-permute-done.14) | copy-start | bytes 3538948
  68.7 99.2 %collective-permute-start.13 = (bf16[2,2,16,9216]{3,2,1,0:T(8,128)(2,1)}, bf16[2,2,16,9216]{3,2,1,0:T(8,128)(2,1)}, u32[]{:S(2)}, u32[]{:S(2)}) collective-permute-start(bf16[2,2,16,9216]{3,2,1,0:T(8,128)(2,1)} %collective-permute-done.12), channel_id=1, source_target_pairs={{0,12},{4,0},{8,4},{12,8},{1,13},{5,1},{9,5},{13,9},{2,14},{6,2},{... | collective-permute-start | bytes 3538952 | tf_op jit(solution)/shard_map/ppermute | solution.py:18
  92.3 79.1 %collective-permute-start.17 = (bf16[2,2,16,9216]{3,2,1,0:T(8,128)(2,1)}, bf16[2,2,16,9216]{3,2,1,0:T(8,128)(2,1)}, u32[]{:S(2)}, u32[]{:S(2)}) collective-permute-start(bf16[2,2,16,9216]{3,2,1,0:T(8,128)(2,1)} %collective-permute-done.16), channel_id=1, source_target_pairs={{0,4},{4,8},{8,12},{12,0},{1,5},{5,9},{9,13},{13,1},{2,6},{6,10},{... | collective-permute-start | bytes 3538952 | tf_op jit(solution)/shard_map/ppermute | solution.py:18
  117.5 57.4 %collective-permute-start.19 = (bf16[2,2,16,9216]{3,2,1,0:T(8,128)(2,1)}, bf16[2,2,16,9216]{3,2,1,0:T(8,128)(2,1)}, u32[]{:S(2)}, u32[]{:S(2)}) collective-permute-start(bf16[2,2,16,9216]{3,2,1,0:T(8,128)(2,1)} %collective-permute-done.18), channel_id=1, source_target_pairs={{0,12},{4,0},{8,4},{12,8},{1,13},{5,1},{9,5},{13,9},{2,14},{6,2},{... | collective-permute-start | bytes 3538952 | tf_op jit(solution)/shard_map/ppermute | solution.py:18
  133.6 6.4 %copy-start.12 = (s32[2,4,16]{2,1,0:T(4,128)S(1)}, s32[2,4,16]{2,1,0:T(4,128)}, u32[]{:S(2)}) copy-start(s32[2,4,16]{2,1,0:T(4,128)} %param.8) | copy-start | bytes 1540
  133.6 7.3 %copy-start.11 = (s32[2,4,16]{2,1,0:T(4,128)S(1)}, s32[2,4,16]{2,1,0:T(4,128)}, u32[]{:S(2)}) copy-start(s32[2,4,16]{2,1,0:T(4,128)} %param.7) | copy-start | bytes 1540
  178.4 1.4 copy-start
  179.8 1.4 copy-start.1
  181.2 1.4 copy-start.2
  182.7 1.4 copy-start.3
  184.1 1.4 copy-start.4
  185.5 1.4 copy-start.5
  186.9 1.4 copy-start.6
  188.3 1.4 copy-start.7
  189.7 1.4 copy-start.8

commit v2 on v1

--- a/solution.py
+++ b/solution.py
@@ -13,36 +13,175 @@
 GROUP = 2
 
 
-def shift(array, axis, step):
-    peers = lax.axis_size(axis)
-    return lax.ppermute(array, axis, [(i, (i + step) % peers) for i in range(peers)])
-
-
-def halo(low, high):
-    own = (low, high)
-    before_x = [shift(p, "col", 1) for p in own]
-    after_x = [shift(p, "col", -1) for p in own]
-    rows = []
-    for mid in (before_x, own, after_x):
-        rows.append([shift(mid[1], "row", 1), mid[0], mid[1], shift(mid[0], "row", -1)])
-    return rows
-
-
-def product_kernel(slots, pieces, *refs):
-    table = refs[0]
-    left = refs[1]
-    sources = refs[2 : 2 + pieces]
-    out = refs[2 + pieces]
-    near, wide_a, wide_b, sems = refs[3 + pieces :]
-    span = near.shape[0] // pieces
-    copies = [
-        pltpu.make_async_copy(src, near.at[pl.ds(n * span, span)], sems.at[n])
-        for n, src in enumerate(sources)
+HALF = BS // 2
+PAIR_ROWS = 3 * HALF
+WIDE = 64
+CHUNKS = 2
+MESH = pl.DeviceIdType.MESH
+
+
+def pack(first, second):
+    parts = [first[:HALF, :WIDE], first[HALF:, :WIDE]]
+    others = [second[:HALF, :WIDE], second[HALF:, :WIDE]]
+    narrow = [t[h : h + HALF, WIDE:] for t in (first, second) for h in (0, HALF)]
+    return [jnp.concatenate(p, axis=1) for p in (parts, others, narrow)]
+
+
+def unpack(rows_0, rows_1, narrow):
+    step = BS - WIDE
+    return [
+        jnp.concatenate(
+            [rows[:, h * WIDE : (h + 1) * WIDE], narrow[:, n * step : (n + 1) * step]], axis=1
+        )
+        for n, (rows, h) in enumerate(((rows_0, 0), (rows_0, 1), (rows_1, 0), (rows_1, 1)))
     ]
-    for copy in copies:
-        copy.start()
-    for copy in copies:
-        copy.wait()
+
+
+def halo_kernel(cells_y, slots, peers_col, peers_row, tiles, codes, near, near_codes, own, *sems):
+    send_sems, recv_sems, code_send, code_recv, local_sems = sems
+    col = lax.axis_index("col")
+    row = lax.axis_index("row")
+    up = {"col": lax.rem(col + 1, peers_col)}
+    down = {"col": lax.rem(col + peers_col - 1, peers_col)}
+    right = {"row": lax.rem(row + 1, peers_row)}
+    back = {"row": lax.rem(row + peers_row - 1, peers_row)}
+
+    barrier = pltpu.get_barrier_semaphore()
+    for peer in (up, down, right, back):
+        pl.semaphore_signal(barrier, inc=1, device_id=peer, device_id_type=MESH)
+
+    pairs = slots // 2
+
+    def pack_half(half):
+        for x in range(REACH):
+            for y in range(REACH):
+                source = (x * cells_y + half * REACH + y) * slots
+                target = (x * REACH + y) * pairs
+
+                def one(p, carry):
+                    blocks = pack(tiles[source + 2 * p], tiles[source + 2 * p + 1])
+                    for n, block in enumerate(blocks):
+                        own[half, target + p, n * HALF : (n + 1) * HALF, :] = block
+                    return carry
+
+                lax.fori_loop(0, pairs, one, 0)
+
+    pack_half(0)
+    pack_half(1)
+    pl.semaphore_wait(barrier, 4)
+
+    first_hop = [(0, 1, 0, up), (2, 1, 0, down), (0, 2, 1, up), (2, 2, 1, down)]
+    side_hop = [(1, 3, 0, back), (1, 0, 1, right)]
+    span = own.shape[1] // CHUNKS
+
+    def move(place, chunk, source, device, count):
+        part = pl.ds(chunk * span, span)
+        return pltpu.make_async_remote_copy(
+            src_ref=source.at[part],
+            dst_ref=near.at[place, part],
+            send_sem=send_sems.at[count],
+            recv_sem=recv_sems.at[place, chunk],
+            device_id=device,
+            device_id_type=MESH,
+        )
+
+    def move_code(place, source, device, count):
+        return pltpu.make_async_remote_copy(
+            src_ref=source,
+            dst_ref=near_codes.at[place],
+            send_sem=code_send.at[count],
+            recv_sem=code_recv.at[place],
+            device_id=device,
+            device_id_type=MESH,
+        )
+
+    code_moves = []
+    for px, py, half, device in first_hop + side_hop:
+        code_moves.append(move_code(px * 4 + py, codes.at[half], device, len(code_moves)))
+    for m in code_moves:
+        m.start()
+
+    moves = []
+    chain = []
+    for px, py, half, device in first_hop:
+        for chunk in range(CHUNKS):
+            m = move(px * 4 + py, chunk, own.at[half], device, len(moves))
+            moves.append(m)
+            chain.append((m, px, py, chunk))
+    order = []
+    for n in range(0, len(first_hop), 2):
+        for chunk in range(CHUNKS):
+            order.append(chain[n * CHUNKS + chunk])
+            order.append(chain[(n + 1) * CHUNKS + chunk])
+    sides = []
+    for chunk in range(CHUNKS):
+        for px, py, half, device in side_hop:
+            m = move(px * 4 + py, chunk, own.at[half], device, len(moves))
+            moves.append(m)
+            sides.append(m)
+    ahead = 4
+    for m, *_ in order[:ahead]:
+        m.start()
+    for m in sides:
+        m.start()
+    locals_ = []
+    for half in range(2):
+        locals_.append(
+            pltpu.make_async_copy(own.at[half], near.at[4 + 1 + half], local_sems.at[half])
+        )
+        locals_.append(
+            pltpu.make_async_copy(codes.at[half], near_codes.at[4 + 1 + half], local_sems.at[2 + half])
+        )
+    for m in locals_:
+        m.start()
+
+    code_forwards = []
+    for n, (px, py, half, device) in enumerate(first_hop):
+        code_moves[n].wait_recv()
+        target, device = ((px * 4 + 3), back) if py == 1 else (px * 4, right)
+        m = move_code(target, near_codes.at[px * 4 + py], device, len(code_moves) + n)
+        m.start()
+        code_forwards.append(m)
+
+    forwards = []
+    for n, (m, px, py, chunk) in enumerate(order):
+        m.wait_recv()
+        target, device = ((px * 4 + 3), back) if py == 1 else (px * 4, right)
+        f = move(target, chunk, near.at[px * 4 + py], device, len(moves) + n)
+        f.start()
+        forwards.append(f)
+        if n + ahead < len(order):
+            order[n + ahead][0].start()
+    for m in sides + forwards + code_moves[4:] + code_forwards:
+        m.wait_recv()
+    for m in moves + forwards + code_moves + code_forwards:
+        m.wait_send()
+    for m in locals_:
+        m.wait()
+
+
+def product_kernel(slots, table, left, packed, out, near, raw, wide_a, wide_b, sems):
+    pieces, pairs = packed.shape[:2]
+
+    def fetch(n):
+        return pltpu.make_async_copy(packed.at[n], raw.at[n % 2], sems.at[n % 2])
+
+    fetch(0).start()
+    for n in range(pieces):
+        if n + 1 < pieces:
+            fetch(n + 1).start()
+        fetch(n).wait()
+
+        def one_pair(p, carry):
+            blocks = [raw[n % 2, p, k * HALF : (k + 1) * HALF, :] for k in range(3)]
+            halves = unpack(*blocks)
+            at = (n * pairs + p) * 2
+            for k, half in enumerate(halves):
+                near[at + k // 2, (k % 2) * HALF : (k % 2 + 1) * HALF, :] = half
+            return carry
+
+        lax.fori_loop(0, pairs, one_pair, 0, unroll=2)
+
     buffers = (wide_a, wide_b)
     rows = left.shape[0]
 
@@ -73,19 +212,44 @@
     cells_x, cells_y, slots, area = left_blocks.shape
     rows = cells_x * cells_y
     assert cells_x == REACH and cells_y == 2 * REACH
-    grid_x = cells_x * lax.axis_size("col")
-    grid_y = cells_y * lax.axis_size("row")
+    peers_col = lax.axis_size("col")
+    peers_row = lax.axis_size("row")
+    grid_x = cells_x * peers_col
+    grid_y = cells_y * peers_row
+    cells = REACH * REACH
+    pieces = 12
+    pairs = cells * slots // 2
+    vmem = pl.BlockSpec(memory_space=pltpu.VMEM)
+    anywhere = pl.BlockSpec(memory_space=pl.ANY)
 
     codes = pattern * 2 + (right_live != 0).astype(jnp.int32)
-    code_pieces = halo(codes[:, :REACH], codes[:, REACH:])
-    tile_pieces = halo(right_blocks[:, :REACH], right_blocks[:, REACH:])
-    cells = REACH * REACH
-    near_codes = jnp.concatenate(
-        [p.reshape(cells, slots) for line in code_pieces for p in line], axis=0
-    )
-    sources = [
-        p.reshape(cells * slots, BS, BS) for line in tile_pieces for p in line
-    ]
+    codes = jnp.stack([codes[:, :REACH], codes[:, REACH:]]).reshape(2, cells, slots)
+    codes = jnp.pad(codes, ((0, 0), (0, 8 - cells), (0, LANES - slots)))
+    count = 6 * CHUNKS + 4 * CHUNKS
+    packed, near_codes = pl.pallas_call(
+        functools.partial(halo_kernel, cells_y, slots, peers_col, peers_row),
+        out_shape=(
+            jax.ShapeDtypeStruct((pieces, pairs, PAIR_ROWS, LANES), jnp.bfloat16),
+            jax.ShapeDtypeStruct((pieces, 8, LANES), jnp.int32),
+        ),
+        in_specs=[vmem, vmem],
+        out_specs=(anywhere, anywhere),
+        scratch_shapes=[
+            pltpu.VMEM((2, pairs, PAIR_ROWS, LANES), jnp.bfloat16),
+            pltpu.SemaphoreType.DMA((count,)),
+            pltpu.SemaphoreType.DMA((pieces, CHUNKS)),
+            pltpu.SemaphoreType.DMA((10,)),
+            pltpu.SemaphoreType.DMA((pieces,)),
+            pltpu.SemaphoreType.DMA((4,)),
+        ],
+        compiler_params=pltpu.CompilerParams(
+            collective_id=0, has_side_effects=True, vmem_limit_bytes=16 * 1024 * 1024
+        ),
+        cost_estimate=pl.CostEstimate(
+            flops=0, bytes_accessed=2 * pieces * cells * slots * area, transcendentals=0
+        ),
+    )(right_blocks.reshape(rows * slots, BS, BS), codes)
+    near_codes = near_codes[:, :cells, :slots].reshape(pieces * cells, slots)
 
     local_x = jnp.arange(cells_x, dtype=jnp.int32)[:, None, None]
     local_y = jnp.arange(cells_y, dtype=jnp.int32)[None, :, None]
@@ -106,27 +270,25 @@
     left = left_blocks.reshape(rows, slots, BS, BS)
     left = jnp.moveaxis(left, 1, 2).reshape(rows, BS, slots * BS)
 
-    count = len(sources)
-    vmem = pl.BlockSpec(memory_space=pltpu.VMEM)
     out = pl.pallas_call(
-        functools.partial(product_kernel, slots, count),
+        functools.partial(product_kernel, slots),
         out_shape=jax.ShapeDtypeStruct((rows, slots, BS, BS), jnp.bfloat16),
-        in_specs=[pl.BlockSpec(memory_space=pltpu.SMEM), vmem]
-        + [pl.BlockSpec(memory_space=pl.ANY)] * count,
+        in_specs=[pl.BlockSpec(memory_space=pltpu.SMEM), vmem, anywhere],
         out_specs=vmem,
         scratch_shapes=[
-            pltpu.VMEM((count * cells * slots, BS, BS), jnp.bfloat16),
+            pltpu.VMEM((pieces * cells * slots, BS, BS), jnp.bfloat16),
+            pltpu.VMEM((2, pairs, PAIR_ROWS, LANES), jnp.bfloat16),
             pltpu.VMEM((slots * BS, GROUP * LANES), jnp.bfloat16),
             pltpu.VMEM((slots * BS, GROUP * LANES), jnp.bfloat16),
-            pltpu.SemaphoreType.DMA((count,)),
+            pltpu.SemaphoreType.DMA((2,)),
         ],
         compiler_params=pltpu.CompilerParams(vmem_limit_bytes=36 * 1024 * 1024),
         cost_estimate=pl.CostEstimate(
             flops=2 * rows * slots * slots * BS**3,
-            bytes_accessed=2 * (count * cells + 2 * rows) * slots * area,
+            bytes_accessed=2 * (pieces * cells + 2 * rows) * slots * area,
             transcendentals=0,
         ),
-    )(table, left, *sources)
+    )(table, left, packed)
     return out.reshape(cells_x, cells_y, slots, area)
 
 

time: 226 us -> 197 us (0.87)
  Pallas kernels: 26.9 us -> 162 us
  waiting for transfers between devices: 93.8 us -> 0 us
  local copies, waits for them, and re-layouts: 80.2 us -> 30.4 us
  starting transfers between devices: 20.3 us -> 0 us
    pallas_call x1 -> x2, Pallas kernels: 26.9 us -> 162 us  [the longest x1 119 us: body(): pl.pallas_call(functools.partial(halo_kernel, cells_y, slots, peers_col,...]
    ppermute x20 -> x0, waiting for transfers between devices: 93.8 us -> none  [shift(): lax.ppermute(array, axis, [(i, (i + step) % peers) for i in range(peers)])]
    reshape x12 -> x1, local copies, waits for them, and re-layouts: 40.2 us -> 4.47 us  [body(): right_blocks.reshape(rows * slots, BS, BS)]
    ppermute x20 -> x0, starting transfers between devices: 20.3 us -> none  [shift(): lax.ppermute(array, axis, [(i, (i + step) % peers) for i in range(peers)])]
    unnamed x26 -> x6, local copies, waits for them, and re-layouts: 12.7 us -> 6.73 us
    slice x2, local copies, waits for them, and re-layouts: 2.88 us -> 0.01 us  [the longest x1 0.01 us: body(): near_codes = near_codes[:, :cells, :slots].reshape(pieces * cells, slots)]
  transfers between devices with their start and end apart: 20 -> 0, of which waited for: 4 -> 0; matrix products, arithmetic and copies ran while one was open for 27% -> 0% of each run, Pallas kernels for 0% -> 0%
where the time goes in v2:
time: 197 us; the launch traced here: 196 us
  Pallas kernels  162 us (82%)
  local copies, waits for them, and re-layouts  30.4 us (15%)
  other arithmetic  4.05 us (2%)
    pallas_call x1, Pallas kernels, body(): pl.pallas_call(functools.partial(halo_kernel, cells_y, slots, peers_col,...  119 us
    pallas_call x1, Pallas kernels, body(): pl.pallas_call(functools.partial(product_kernel, slots), out_shape=jax.Sh...  42.3 us
    reshape x2, local copies, waits for them, and re-layouts, body(): left = left_blocks.reshape(rows, slots, BS, BS)  8.77 us
    unnamed x6, local copies, waits for them, and re-layouts  6.73 us
    reshape x1, local copies, waits for them, and re-layouts, body(): return out.reshape(cells_x, cells_y, slots, area)  5.09 us
    reshape x1, local copies, waits for them, and re-layouts, body(): left = jnp.moveaxis(left, 1, 2).reshape(rows, BS, slots * BS)  4.48 us
    reshape x1, local copies, waits for them, and re-layouts, body(): right_blocks.reshape(rows * slots, BS, BS)  4.47 us

profile of v2, /device:TPU:0, one launch (start us, length us, event | category | flops | bytes accessed | tf_op | source)
XLA Modules:
  0.0 196.2 jit_solution(10304085773067661189)
XLA Ops:
  0.0 0.7 broadcast_compare_fusion
  0.7 0.8 broadcast_multiply_fusion
  1.5 0.1 reshape.147
  1.6 5.7 %reshape.142 = bf16[8,16,96,96]{3,2,1,0:T(8,128)(2,1)} reshape(bf16[2,4,16,9216]{3,2,1,0:T(8,128)(2,1)} %param.5) | data formatting | bytes 4718592 | tf_op jit(solution)/shard_map/reshape | solution.py:270
  7.3 3.1 %copy.10 = bf16[8,16,96,96]{3,1,2,0:T(8,128)(2,1)S(1)} copy(bf16[8,16,96,96]{3,2,1,0:T(8,128)(2,1)} %reshape.142) | data formatting | bytes 4718592 | tf_op jit(solution)/shard_map/reshape | solution.py:270
  10.4 4.5 %reshape.143.left = bf16[8,96,1536]{2,1,0:T(8,128)(2,1)} reshape(bf16[8,96,16,96]{3,2,1,0:T(8,128)(2,1)S(1)} %bitcast.21) | data formatting | bytes 4718592 | tf_op jit(solution)/shard_map/reshape | solution.py:271
  14.9 4.5 %reshape.139.tiles = bf16[128,96,96]{2,1,0:T(8,128)(2,1)S(1)} reshape(bf16[2,4,16,9216]{3,2,1,0:T(8,128)(2,1)} %param.6) | data formatting | bytes 4718592 | tf_op jit(solution)/shard_map/reshape | solution.py:251
  19.4 0.0 copy-start.2
  19.4 119.3 %shard_map.55 = (bf16[12,32,144,128]{3,2,1,0:T(8,128)(2,1)S(1)}, s32[12,8,128]{2,1,0:T(8,128)S(1)}) custom-call(bf16[128,96,96]{2,1,0:T(8,128)(2,1)S(1)} %reshape.139.tiles, s32[2,8,128]{2,1,0:T(8,128)S(1)} %pad.4.codes), custom_call_target="tpu_custom_call" | custom-call | bytes 14155776 | tf_op jit(solution)/shard_map/pallas_call | solution.py:229
  138.7 0.0 copy-start
  138.8 5.1 %copy-done = bf16[12,32,144,128]{3,2,1,0:T(8,128)(2,1)} copy-done((bf16[12,32,144,128]{3,2,1,0:T(8,128)(2,1)}, bf16[12,32,144,128]{3,2,1,0:T(8,128)(2,1)S(1)}, u32[]{:S(2)}) %copy-start) | copy-done | bytes 14155800
  143.8 0.6 gather_fusion
  144.5 0.1 fusion.2
  144.6 0.0 copy-done.2
  144.6 2.3 %select_reduce_fusion = s32[8,16,16]{2,1,0:T(8,128)S(1)} fusion(s32[16]{0:T(128)S(1)} %iota_add_fusion, s32[8,16]{1,0:T(8,128)S(1)} %bitcast.25, s32[8,16,16]{2,1,0:T(8,128)S(1)} %add_select_fusion.1, pred[8,16,16]{2,1,0:T(8,128)(4,1)S(1)} %fusion.2), kind=kLoop, calls=%fused_computation.2 | loop fusion | flops 129024 | bytes 19008 | tf_op jit(solution)/shard_map/reduce_max | solution.py:267
  146.9 0.1 add_select_fusion.2
  147.0 0.1 select_n.89.table
  147.1 0.0 copy-start.1
  147.1 1.7 copy-done.1
  148.8 42.3 %shard_map.56 = bf16[8,16,96,96]{3,2,1,0:T(8,128)(2,1)S(1)} custom-call(s32[2048]{0:T(1024)S(1)} %select_n.89.table, bf16[8,96,1536]{2,1,0:T(8,128)(2,1)S(1)} %copy-done.1, bf16[12,32,144,128]{3,2,1,0:T(8,128)(2,1)} %copy-done), custom_call_target="tpu_custom_call" | custom-call | flops 3623878656 | bytes 18874368 | tf_op jit(solution)/shard_map/pallas_call | solution.py:273
  191.1 5.1 %reshape.144 = bf16[2,4,16,9216]{3,2,1,0:T(8,128)(2,1)} reshape(bf16[8,16,96,96]{3,2,1,0:T(8,128)(2,1)S(1)} %shard_map.56) | data formatting | bytes 4718592 | tf_op jit(solution)/shard_map/reshape | solution.py:292
  (10 shorter events, 0.1 us)
Async XLA Ops:
  19.4 125.2 %copy-start.2 = (s32[2,4,16]{2,1,0:T(4,128)S(1)}, s32[2,4,16]{2,1,0:T(4,128)}, u32[]{:S(2)}) copy-start(s32[2,4,16]{2,1,0:T(4,128)} %param.7) | copy-start | bytes 1540
  138.7 5.1 %copy-start = (bf16[12,32,144,128]{3,2,1,0:T(8,128)(2,1)}, bf16[12,32,144,128]{3,2,1,0:T(8,128)(2,1)S(1)}, u32[]{:S(2)}) copy-start(bf16[12,32,144,128]{3,2,1,0:T(8,128)(2,1)S(1)} %get-tuple-element.8.packed) | copy-start | bytes 42467332
  147.1 1.7 copy-start.1

commit v3 on v2

v3 whole, which is shorter than its diff:
```python
import functools

import jax
import jax.numpy as jnp
from jax import lax
from jax.experimental import pallas as pl
from jax.experimental.pallas import tpu as pltpu
from jax.sharding import PartitionSpec as P

BS = 96
LANES = 128
REACH = 2
GROUP = 2


HALF = BS // 2
PAIR_ROWS = 3 * HALF
WIDE = 64
CHUNKS = 2
MESH = pl.DeviceIdType.MESH


def pack(first, second):
    parts = [first[:HALF, :WIDE], first[HALF:, :WIDE]]
    others = [second[:HALF, :WIDE], second[HALF:, :WIDE]]
    narrow = [t[h : h + HALF, WIDE:] for t in (first, second) for h in (0, HALF)]
    return [jnp.concatenate(p, axis=1) for p in (parts, others, narrow)]


def unpack(rows_0, rows_1, narrow):
    step = BS - WIDE
    return [
        jnp.concatenate(
            [rows[:, h * WIDE : (h + 1) * WIDE], narrow[:, n * step : (n + 1) * step]], axis=1
        )
        for n, (rows, h) in enumerate(((rows_0, 0), (rows_0, 1), (rows_1, 0), (rows_1, 1)))
    ]


def near_kernel(
    cells_y, slots, peers_col, peers_row,
    place, tiles, left, codes, targets,
    out,
    packed, near, near_codes, table_rows, table, stacked, wide_a, wide_b, *sems,
):
    send_sems, recv_sems, code_send, code_recv, table_sem = sems
    col = lax.axis_index("col")
    row = lax.axis_index("row")
    up = {"col": lax.rem(col + 1, peers_col)}
    down = {"col": lax.rem(col + peers_col - 1, peers_col)}
    right = {"row": lax.rem(row + 1, peers_row)}
    back = {"row": lax.rem(row + peers_row - 1, peers_row)}
    pairs = slots // 2
    piece_pairs = packed.shape[1]
    span = piece_pairs // CHUNKS
    cells = REACH * REACH
    rows = out.shape[0]

    barrier = pltpu.get_barrier_semaphore()
    for peer in (up, down, right, back):
        pl.semaphore_signal(barrier, inc=1, device_id=peer, device_id_type=MESH)

    def pack_half(half):
        for x in range(REACH):
            for y in range(REACH):
                source = (x * cells_y + half * REACH + y) * slots
                target = (x * REACH + y) * pairs

                def one(p, carry):
                    first, second = tiles[source + 2 * p], tiles[source + 2 * p + 1]
                    for n, block in enumerate(pack(first, second)):
                        packed[5 + half, target + p, n * HALF : (n + 1) * HALF, :] = block
                    at = ((5 + half) * piece_pairs + target + p) * 2
                    near[at] = first
                    near[at + 1] = second
                    return carry

                lax.fori_loop(0, pairs, one, 0)

    def unpack_chunk(at_piece, chunk):
        def one(p, carry):
            blocks = [
                packed[at_piece, chunk * span + p, k * HALF : (k + 1) * HALF, :] for k in range(3)
            ]
            at = (at_piece * piece_pairs + chunk * span + p) * 2
            for k, half in enumerate(unpack(*blocks)):
                near[at + k // 2, (k % 2) * HALF : (k % 2 + 1) * HALF, :] = half
            return carry

        lax.fori_loop(0, span, one, 0)

    def move(to, chunk, source, device, count):
        part = pl.ds(chunk * span, span)
        return pltpu.make_async_remote_copy(
            src_ref=packed.at[source, part],
            dst_ref=packed.at[to, part],
            send_sem=send_sems.at[count],
            recv_sem=recv_sems.at[to, chunk],
            device_id=device,
            device_id_type=MESH,
        )

    def move_code(to, source, device, count):
        return pltpu.make_async_remote_copy(
            src_ref=source,
            dst_ref=near_codes.at[pl.ds(to * cells, cells)],
            send_sem=code_send.at[count],
            recv_sem=code_recv.at[to],
            device_id=device,
            device_id_type=MESH,
        )

    first_hop = [(0, 1, 0, up), (2, 1, 0, down), (0, 2, 1, up), (2, 2, 1, down)]
    side_hop = [(1, 3, 0, back), (1, 0, 1, right)]
    code_moves = []
    for px, py, half, device in first_hop + side_hop:
        code_moves.append(move_code(px * 4 + py, codes.at[half], device, len(code_moves)))
    moves = []
    order = []
    for n in range(0, len(first_hop), 2):
        for chunk in range(CHUNKS):
            for px, py, half, device in first_hop[n : n + 2]:
                m = move(px * 4 + py, chunk, 5 + half, device, len(moves))
                moves.append(m)
                order.append((m, px, py, chunk))
    sides = []
    for px, py, half, device in side_hop:
        for chunk in range(CHUNKS):
            m = move(px * 4 + py, chunk, 5 + half, device, len(moves))
            moves.append(m)
            sides.append((m, px * 4 + py, chunk))

    pack_half(0)
    pl.semaphore_wait(barrier, 4)
    ahead = 2 * CHUNKS
    for m in code_moves:
        m.start()
    for m, *_ in order[:ahead]:
        m.start()
    for m, *_ in sides[:CHUNKS]:
        m.start()
    pack_half(1)
    for m, *_ in sides[CHUNKS:]:
        m.start()

    def stack_row(i, carry):
        for g in range(0, slots, 4):
            parts = [left[i * slots + g + u] for u in range(4)]
            stacked[i, :, g * BS : (g + 4) * BS] = jnp.concatenate(parts, axis=1)
        return carry

    near_codes[5 * cells : 7 * cells] = codes[...].reshape(2 * cells, *codes.shape[2:])
    code_forwards = []
    for n, (px, py, half, device) in enumerate(first_hop):
        code_moves[n].wait_recv()
        to, device = ((px * 4 + 3), back) if py == 1 else (px * 4, right)
        source = near_codes.at[pl.ds((px * 4 + py) * cells, cells)]
        m = move_code(to, source, device, len(code_moves) + n)
        m.start()
        code_forwards.append(m)
    lax.fori_loop(0, rows, stack_row, 0)
    for m in code_moves[4:] + code_forwards:
        m.wait_recv()

    slot_rows = lax.broadcasted_iota(jnp.int32, (slots, LANES), 0)

    def table_row(n, carry):
        at = place[n]
        held = near_codes[jnp.maximum(at, 0)]
        match = (lax.shift_right_logical(held, 1) == targets[n // slots]) & ((held & 1) == 1)
        found = jnp.max(jnp.where(match, slot_rows + 1, 0), axis=0, keepdims=True)
        good = (found > 0) & (at >= 0)
        table_rows[pl.ds(n, 1)] = jnp.where(good, at * slots + found - 1, -1)
        return carry

    lax.fori_loop(0, rows * slots, table_row, 0)
    table_copy = pltpu.make_async_copy(table_rows, table, table_sem)
    table_copy.start()

    forwards = []
    for n, (m, px, py, chunk) in enumerate(order):
        m.wait_recv()
        to, device = ((px * 4 + 3), back) if py == 1 else (px * 4, right)
        f = move(to, chunk, px * 4 + py, device, len(moves) + n)
        f.start()
        forwards.append((f, to, chunk))
        if n + ahead < len(order):
            order[n + ahead][0].start()
        unpack_chunk(px * 4 + py, chunk)
        if n < len(sides):
            sides[n][0].wait_recv()
            unpack_chunk(*sides[n][1:])
        if n >= 2:
            forwards[n - 2][0].wait_recv()
            unpack_chunk(*forwards[n - 2][1:])
    for f, to, chunk in forwards[-2:]:
        f.wait_recv()
        unpack_chunk(to, chunk)
    table_copy.wait()

    buffers = (wide_a, wide_b)

    def gather(i, first, wide):
        for g in range(slots):
            for u in range(GROUP):
                at = table[i * slots + g, first + u]
                tile = near[jnp.maximum(at, 0)]
                tile = jnp.where(at >= 0, tile, jnp.zeros_like(tile))
                wide[g * BS : (g + 1) * BS, u * LANES : u * LANES + BS] = tile

    def one_row(i, carry):
        lhs = stacked[i]
        for turn in range(slots // GROUP):
            wide = buffers[turn % 2]
            gather(i, turn * GROUP, wide)
            total = jnp.dot(lhs, wide[...], preferred_element_type=jnp.float32)
            total = (0.5 * total).astype(out.dtype)
            for u in range(GROUP):
                out[i, turn * GROUP + u] = total[:, u * LANES : u * LANES + BS]
        return carry

    wide_a[...] = jnp.zeros_like(wide_a)
    wide_b[...] = jnp.zeros_like(wide_b)
    lax.fori_loop(0, rows, one_row, 0)
    for m in moves + [f for f, *_ in forwards] + code_moves + code_forwards:
        m.wait_send()


def body(left_blocks, right_blocks, pattern, left_live, right_live):
    cells_x, cells_y, slots, area = left_blocks.shape
    rows = cells_x * cells_y
    assert cells_x == REACH and cells_y == 2 * REACH
    peers_col = lax.axis_size("col")
    peers_row = lax.axis_size("row")
    grid_x = cells_x * peers_col
    grid_y = cells_y * peers_row
    cells = REACH * REACH
    pieces = 12
    piece_pairs = cells * slots // 2
    vmem = pl.BlockSpec(memory_space=pltpu.VMEM)

    codes = pattern * 2 + (right_live != 0).astype(jnp.int32)
    codes = jnp.stack([codes[:, :REACH], codes[:, REACH:]]).reshape(2, cells, slots, 1)
    codes = jnp.broadcast_to(codes, (2, cells, slots, LANES))

    local_x = jnp.arange(cells_x, dtype=jnp.int32)[:, None, None]
    local_y = jnp.arange(cells_y, dtype=jnp.int32)[None, :, None]
    own_x = lax.axis_index("col") * cells_x + local_x
    own_y = lax.axis_index("row") * cells_y + local_y
    near_x = local_x + (pattern // grid_y - own_x + REACH) % grid_x
    near_y = local_y + (pattern % grid_y - own_y + REACH) % grid_y
    piece = (near_x // REACH) * 4 + near_y // REACH
    place = piece * cells + (near_x % REACH) * REACH + near_y % REACH
    place = jnp.where(left_live != 0, place, -1).reshape(-1)
    targets = jnp.pad(
        pattern.reshape(rows, 1, slots), ((0, 0), (0, 0), (0, LANES - slots)), constant_values=-1
    )

    count = 10 * CHUNKS
    out = pl.pallas_call(
        functools.partial(near_kernel, cells_y, slots, peers_col, peers_row),
        out_shape=jax.ShapeDtypeStruct((rows, slots, BS, BS), jnp.bfloat16),
        in_specs=[pl.BlockSpec(memory_space=pltpu.SMEM), vmem, vmem, vmem, vmem],
        out_specs=vmem,
        scratch_shapes=[
            pltpu.VMEM((pieces, piece_pairs, PAIR_ROWS, LANES), jnp.bfloat16),
            pltpu.VMEM((pieces * cells * slots, BS, BS), jnp.bfloat16),
            pltpu.VMEM((pieces * cells, slots, LANES), jnp.int32),
            pltpu.VMEM((rows * slots, LANES), jnp.int32),
            pltpu.SMEM((rows * slots, LANES), jnp.int32),
            pltpu.VMEM((rows, BS, slots * BS), jnp.bfloat16),
            pltpu.VMEM((slots * BS, GROUP * LANES), jnp.bfloat16),
            pltpu.VMEM((slots * BS, GROUP * LANES), jnp.bfloat16),
            pltpu.SemaphoreType.DMA((count,)),
            pltpu.SemaphoreType.DMA((pieces, CHUNKS)),
            pltpu.SemaphoreType.DMA((10,)),
            pltpu.SemaphoreType.DMA((pieces,)),
            pltpu.SemaphoreType.DMA,
        ],
        compiler_params=pltpu.CompilerParams(
            collective_id=0, has_side_effects=True, vmem_limit_bytes=56 * 1024 * 1024
        ),
        cost_estimate=pl.CostEstimate(
            flops=2 * rows * slots * slots * BS**3,
            bytes_accessed=6 * rows * slots * area,
            transcendentals=0,
        ),
    )(
        place,
        right_blocks.reshape(rows * slots, BS, BS),
        left_blocks.reshape(rows * slots, BS, BS),
        codes,
        targets,
    )
    return out.reshape(cells_x, cells_y, slots, area)


def solution(mesh):
    placed = (
        P(("win", "col"), "row", None, None),
        P(("win", "col"), "row", None, None),
        P(("win", "col"), "row", None),
        P(("win", "col"), "row", None),
        P(("win", "col"), "row", None),
    )
    return jax.shard_map(
        body,
        mesh=mesh,
        in_specs=placed,
        out_specs=P(("win", "col"), "row", None, None),
        check_vma=False,
    )
```

time: 197 us -> 167 us (0.85)
  Pallas kernels: 162 us -> 146 us
  local copies, waits for them, and re-layouts: 30.4 us -> 19.3 us
  other arithmetic: 4.05 us -> 0.83 us
    pallas_call x2 -> x1, Pallas kernels: 162 us -> 146 us  [body(): pl.pallas_call(functools.partial(near_kernel, cells_y, slots, peers_col,...]
    reshape x3 -> x2, local copies, waits for them, and re-layouts: 13.3 us -> 6.35 us  [the longest x1 5.7 us: body(): left_blocks.reshape(rows * slots, BS, BS)]
    unnamed x6 -> x2, local copies, waits for them, and re-layouts: 6.73 us -> 0.01 us
    reduce_max x1 -> x0, other arithmetic: 2.31 us -> none  [body(): jnp.where(match, jnp.arange(slots, dtype=jnp.int32) + 1, 0).max(axis=3)]
where the time goes in v3:
time: 167 us
  Pallas kernels  146 us (87%)
  local copies, waits for them, and re-layouts  19.3 us (12%)
    pallas_call x1, Pallas kernels, body(): pl.pallas_call(functools.partial(near_kernel, cells_y, slots, peers_col,...  146 us
    reshape x1, local copies, waits for them, and re-layouts, body(): return out.reshape(cells_x, cells_y, slots, area)  6.69 us
    reshape x1, local copies, waits for them, and re-layouts, body(): left_blocks.reshape(rows * slots, BS, BS)  5.7 us
    reshape x1, local copies, waits for them, and re-layouts, body(): right_blocks.reshape(rows * slots, BS, BS)  4.12 us

profile of v3, /device:TPU:0, one launch (start us, length us, event | category | flops | bytes accessed | tf_op | source)
XLA Modules:
  0.0 166.6 jit_solution(10844260027639387592)
XLA Ops:
  0.0 0.0 copy-start
  0.0 1.4 pad.4.targets
  1.4 0.8 convert_add_fusion
  2.3 0.7 reshape.30.place
  2.9 0.7 broadcast_in_dim.12.codes
  3.6 5.7 %reshape.32.left = bf16[128,96,96]{2,1,0:T(8,128)(2,1)} reshape(bf16[2,4,16,9216]{3,2,1,0:T(8,128)(2,1)} %param.5) | data formatting | bytes 4718592 | tf_op jit(solution)/shard_map/reshape | solution.py:291
  9.3 0.0 copy-done
  9.3 4.1 %reshape.31.tiles = bf16[128,96,96]{2,1,0:T(8,128)(2,1)} reshape(bf16[2,4,16,9216]{3,2,1,0:T(8,128)(2,1)S(1)} %copy-done) | data formatting | bytes 4718592 | tf_op jit(solution)/shard_map/reshape | solution.py:290
  13.5 146.4 %shard_map.55 = bf16[8,16,96,96]{3,2,1,0:T(8,128)(2,1)} custom-call(s32[128]{0:T(128)} %reshape.30.place, bf16[128,96,96]{2,1,0:T(8,128)(2,1)} %reshape.31.tiles, bf16[128,96,96]{2,1,0:T(8,128)(2,1)} %reshape.32.left, s32[2,4,16,128]{3,2,1,0:T(8,128)} %broadcast_in_dim.12.codes, s32[8,1,128]{2,1,0:T(1,128)} %pad.4.targets), custom_call_target="tpu_custom_call" | custom-call | flops 3623878656 | bytes 7077888 | tf_op jit(solution)/shard_map/pallas_call | solution.py:260
  159.9 6.7 %reshape.34 = bf16[2,4,16,9216]{3,2,1,0:T(8,128)(2,1)} reshape(bf16[8,16,96,96]{3,2,1,0:T(8,128)(2,1)} %shard_map.55) | data formatting | bytes 4718592 | tf_op jit(solution)/shard_map/reshape | solution.py:295
  (4 shorter events, 0.0 us)
Async XLA Ops:
  0.0 9.3 %copy-start = (bf16[2,4,16,9216]{3,2,1,0:T(8,128)(2,1)S(1)}, bf16[2,4,16,9216]{3,2,1,0:T(8,128)(2,1)}, u32[]{:S(2)}) copy-start(bf16[2,4,16,9216]{3,2,1,0:T(8,128)(2,1)} %param.6) | copy-start | bytes 7077892

commit v4 on v3

--- a/solution.py
+++ b/solution.py
@@ -39,9 +39,9 @@
 
 def near_kernel(
     cells_y, slots, peers_col, peers_row,
-    place, tiles, left, codes, targets,
+    place, turn_of, tiles, left, codes, targets,
     out,
-    packed, near, near_codes, table_rows, table, stacked, wide_a, wide_b, *sems,
+    packed, near, near_codes, table_rows, table, stacked, partial, wide_a, wide_b, *sems,
 ):
     send_sems, recv_sems, code_send, code_recv, table_sem = sems
     col = lax.axis_index("col")
@@ -143,11 +143,30 @@
     for m, *_ in sides[CHUNKS:]:
         m.start()
 
-    def stack_row(i, carry):
-        for g in range(0, slots, 4):
-            parts = [left[i * slots + g + u] for u in range(4)]
-            stacked[i, :, g * BS : (g + 4) * BS] = jnp.concatenate(parts, axis=1)
-        return carry
+    late_counts = (9, 6)
+
+    def row_of(j, kind):
+        return (j // REACH) * cells_y + kind * REACH + j % REACH
+
+    def spans(kind):
+        late = late_counts[kind]
+        start = -(-late * BS // LANES) * LANES
+        return ((0, late, 0), (late, slots, start))
+
+    def stack_rows(kind):
+        def one(j, carry):
+            i = row_of(j, kind)
+            for first, last, start in spans(kind):
+                for g in range(first, last, 4):
+                    parts = [
+                        left[i * slots + turn_of[i * slots + u]] for u in range(g, min(g + 4, last))
+                    ]
+                    at = start + (g - first) * BS
+                    block = parts[0] if len(parts) == 1 else jnp.concatenate(parts, axis=1)
+                    stacked[i, :, at : at + len(parts) * BS] = block
+            return carry
+
+        lax.fori_loop(0, rows // 2, one, 0)
 
     near_codes[5 * cells : 7 * cells] = codes[...].reshape(2 * cells, *codes.shape[2:])
     code_forwards = []
@@ -158,7 +177,8 @@
         m = move_code(to, source, device, len(code_moves) + n)
         m.start()
         code_forwards.append(m)
-    lax.fori_loop(0, rows, stack_row, 0)
+    stack_rows(0)
+    stack_rows(1)
     for m in code_moves[4:] + code_forwards:
         m.wait_recv()
 
@@ -177,6 +197,37 @@
     table_copy = pltpu.make_async_copy(table_rows, table, table_sem)
     table_copy.start()
 
+    buffers = (wide_a, wide_b)
+
+    def product_rows(kind, early):
+        first, last, start = spans(kind)[early]
+        depth = (last - first) * BS
+
+        def one(j, carry):
+            i = row_of(j, kind)
+            lhs = stacked[i, :, start : start + depth]
+            for turn in range(slots // GROUP):
+                wide = buffers[turn % 2]
+                for g in range(first, last):
+                    for u in range(GROUP):
+                        at = table[i * slots + g, turn * GROUP + u]
+                        tile = near[jnp.maximum(at, 0)]
+                        tile = jnp.where(at >= 0, tile, jnp.zeros_like(tile))
+                        down_to = (g - first) * BS
+                        wide[down_to : down_to + BS, u * LANES : u * LANES + BS] = tile
+                total = jnp.dot(lhs, wide[:depth], preferred_element_type=jnp.float32)
+                if early:
+                    partial[i, turn] = total
+                else:
+                    total = (0.5 * (total + partial[i, turn])).astype(out.dtype)
+                    for u in range(GROUP):
+                        out[i, turn * GROUP + u] = total[:, u * LANES : u * LANES + BS]
+            return carry
+
+        lax.fori_loop(0, rows // 2, one, 0)
+
+    wide_a[...] = jnp.zeros_like(wide_a)
+    wide_b[...] = jnp.zeros_like(wide_b)
     forwards = []
     for n, (m, px, py, chunk) in enumerate(order):
         m.wait_recv()
@@ -193,35 +244,16 @@
         if n >= 2:
             forwards[n - 2][0].wait_recv()
             unpack_chunk(*forwards[n - 2][1:])
+        if n == 2 * CHUNKS + 1:
+            table_copy.wait()
+            product_rows(0, 1)
+        if n == 2 * CHUNKS + 2:
+            product_rows(1, 1)
     for f, to, chunk in forwards[-2:]:
         f.wait_recv()
         unpack_chunk(to, chunk)
-    table_copy.wait()
-
-    buffers = (wide_a, wide_b)
-
-    def gather(i, first, wide):
-        for g in range(slots):
-            for u in range(GROUP):
-                at = table[i * slots + g, first + u]
-                tile = near[jnp.maximum(at, 0)]
-                tile = jnp.where(at >= 0, tile, jnp.zeros_like(tile))
-                wide[g * BS : (g + 1) * BS, u * LANES : u * LANES + BS] = tile
-
-    def one_row(i, carry):
-        lhs = stacked[i]
-        for turn in range(slots // GROUP):
-            wide = buffers[turn % 2]
-            gather(i, turn * GROUP, wide)
-            total = jnp.dot(lhs, wide[...], preferred_element_type=jnp.float32)
-            total = (0.5 * total).astype(out.dtype)
-            for u in range(GROUP):
-                out[i, turn * GROUP + u] = total[:, u * LANES : u * LANES + BS]
-        return carry
-
-    wide_a[...] = jnp.zeros_like(wide_a)
-    wide_b[...] = jnp.zeros_like(wide_b)
-    lax.fori_loop(0, rows, one_row, 0)
+    product_rows(0, 0)
+    product_rows(1, 0)
     for m in moves + [f for f, *_ in forwards] + code_moves + code_forwards:
         m.wait_send()
 
@@ -251,7 +283,13 @@
     near_y = local_y + (pattern % grid_y - own_y + REACH) % grid_y
     piece = (near_x // REACH) * 4 + near_y // REACH
     place = piece * cells + (near_x % REACH) * REACH + near_y % REACH
-    place = jnp.where(left_live != 0, place, -1).reshape(-1)
+    last = (piece // 4 != 1) & (piece % 2 == 0)
+    key = jnp.where(last, 0, slots).reshape(rows, slots) + jnp.arange(slots, dtype=jnp.int32)
+    rank = jnp.sum(key[:, None, :] < key[:, :, None], axis=2, dtype=jnp.int32)
+    hit = rank[:, None, :] == jnp.arange(slots, dtype=jnp.int32)[None, :, None]
+    turn_of = jnp.where(hit, jnp.arange(slots, dtype=jnp.int32), 0).sum(axis=2).reshape(-1)
+    place = jnp.where(left_live != 0, place, -1).reshape(rows, 1, slots)
+    place = jnp.where(hit, place, 0).sum(axis=2).reshape(-1)
     targets = jnp.pad(
         pattern.reshape(rows, 1, slots), ((0, 0), (0, 0), (0, LANES - slots)), constant_values=-1
     )
@@ -260,7 +298,7 @@
     out = pl.pallas_call(
         functools.partial(near_kernel, cells_y, slots, peers_col, peers_row),
         out_shape=jax.ShapeDtypeStruct((rows, slots, BS, BS), jnp.bfloat16),
-        in_specs=[pl.BlockSpec(memory_space=pltpu.SMEM), vmem, vmem, vmem, vmem],
+        in_specs=[pl.BlockSpec(memory_space=pltpu.SMEM)] * 2 + [vmem] * 4,
         out_specs=vmem,
         scratch_shapes=[
             pltpu.VMEM((pieces, piece_pairs, PAIR_ROWS, LANES), jnp.bfloat16),
@@ -268,7 +306,8 @@
             pltpu.VMEM((pieces * cells, slots, LANES), jnp.int32),
             pltpu.VMEM((rows * slots, LANES), jnp.int32),
             pltpu.SMEM((rows * slots, LANES), jnp.int32),
-            pltpu.VMEM((rows, BS, slots * BS), jnp.bfloat16),
+            pltpu.VMEM((rows, BS, slots * BS + LANES), jnp.bfloat16),
+            pltpu.VMEM((rows, slots // GROUP, BS, GROUP * LANES), jnp.float32),
             pltpu.VMEM((slots * BS, GROUP * LANES), jnp.bfloat16),
             pltpu.VMEM((slots * BS, GROUP * LANES), jnp.bfloat16),
             pltpu.SemaphoreType.DMA((count,)),
@@ -278,7 +317,7 @@
             pltpu.SemaphoreType.DMA,
         ],
         compiler_params=pltpu.CompilerParams(
-            collective_id=0, has_side_effects=True, vmem_limit_bytes=56 * 1024 * 1024
+            collective_id=0, has_side_effects=True, vmem_limit_bytes=58 * 1024 * 1024
         ),
         cost_estimate=pl.CostEstimate(
             flops=2 * rows * slots * slots * BS**3,
@@ -287,6 +326,7 @@
         ),
     )(
         place,
+        turn_of,
         right_blocks.reshape(rows * slots, BS, BS),
         left_blocks.reshape(rows * slots, BS, BS),
         codes,

time: 167 us -> 158 us (0.946)
  Pallas kernels: 146 us -> 136 us
    pallas_call x1, Pallas kernels: 146 us -> 136 us  [body(): pl.pallas_call(functools.partial(near_kernel, cells_y, slots, peers_col,...]
where the time goes in v4:
time: 158 us; the launch traced here: 157 us
  Pallas kernels  136 us (86%)
  local copies, waits for them, and re-layouts  20 us (13%)
    pallas_call x1, Pallas kernels, body(): pl.pallas_call(functools.partial(near_kernel, cells_y, slots, peers_col,...  136 us
    reshape x1, local copies, waits for them, and re-layouts, body(): return out.reshape(cells_x, cells_y, slots, area)  6.69 us
    reshape x1, local copies, waits for them, and re-layouts, body(): left_blocks.reshape(rows * slots, BS, BS)  5.71 us
    reshape x1, local copies, waits for them, and re-layouts, body(): right_blocks.reshape(rows * slots, BS, BS)  4.13 us

profile of v4, /device:TPU:0, one launch (start us, length us, event | category | flops | bytes accessed | tf_op | source)
XLA Modules:
  0.0 157.5 jit_solution(4641094518849556969)
XLA Ops:
  0.0 0.0 copy-start
  0.0 1.4 pad.4.targets
  1.4 0.8 fusion.16
  2.3 0.3 convert_reduce_fusion
  2.6 0.4 select_reduce_fusion
  2.9 0.7 reshape.61.turn_of
  3.6 0.7 reshape.60.place
  4.3 0.7 broadcast_in_dim.45.codes
  5.0 5.7 %reshape.63.left = bf16[128,96,96]{2,1,0:T(8,128)(2,1)} reshape(bf16[2,4,16,9216]{3,2,1,0:T(8,128)(2,1)} %param.5) | data formatting | bytes 4718592 | tf_op jit(solution)/shard_map/reshape | solution.py:331
  10.7 0.0 copy-done
  10.7 4.1 %reshape.62.tiles = bf16[128,96,96]{2,1,0:T(8,128)(2,1)} reshape(bf16[2,4,16,9216]{3,2,1,0:T(8,128)(2,1)S(1)} %copy-done) | data formatting | bytes 4718592 | tf_op jit(solution)/shard_map/reshape | solution.py:330
  14.8 136.0 %shard_map.55 = bf16[8,16,96,96]{3,2,1,0:T(8,128)(2,1)} custom-call(s32[128]{0:T(128)} %reshape.60.place, s32[128]{0:T(128)} %reshape.61.turn_of, bf16[128,96,96]{2,1,0:T(8,128)(2,1)} %reshape.62.tiles, bf16[128,96,96]{2,1,0:T(8,128)(2,1)} %reshape.63.left, s32[2,4,16,128]{3,2,1,0:T(8,128)} %broadcast_in_dim.45.codes, s32[8,1,128]{2,1,0:T(1,128)} %pad.4.targets), custom_call_target="tpu_custom_call" | custom-call | flops 3623878656 | bytes 7077888 | tf_op jit(solution)/shard_map/pallas_call | solution.py:298
  150.8 6.7 %reshape.65 = bf16[2,4,16,9216]{3,2,1,0:T(8,128)(2,1)} reshape(bf16[8,16,96,96]{3,2,1,0:T(8,128)(2,1)} %shard_map.55) | data formatting | bytes 4718592 | tf_op jit(solution)/shard_map/reshape | solution.py:335
  (6 shorter events, 0.0 us)
Async XLA Ops:
  0.0 10.7 %copy-start = (bf16[2,4,16,9216]{3,2,1,0:T(8,128)(2,1)S(1)}, bf16[2,4,16,9216]{3,2,1,0:T(8,128)(2,1)}, u32[]{:S(2)}) copy-start(bf16[2,4,16,9216]{3,2,1,0:T(8,128)(2,1)} %param.6) | copy-start | bytes 7077892

commit v5 on v4

--- a/solution.py
+++ b/solution.py
@@ -16,7 +16,7 @@
 HALF = BS // 2
 PAIR_ROWS = 3 * HALF
 WIDE = 64
-CHUNKS = 2
+CHUNKS = 4
 MESH = pl.DeviceIdType.MESH
 
 

time: 158 us -> 154 us (0.975)
  Pallas kernels: 136 us -> 133 us
    pallas_call x1, Pallas kernels: 136 us -> 133 us  [body(): pl.pallas_call(functools.partial(near_kernel, cells_y, slots, peers_col,...]
where the time goes in v5:
time: 154 us
  Pallas kernels  133 us (86%)
  local copies, waits for them, and re-layouts  20 us (13%)
    pallas_call x1, Pallas kernels, body(): pl.pallas_call(functools.partial(near_kernel, cells_y, slots, peers_col,...  133 us
    reshape x1, local copies, waits for them, and re-layouts, body(): return out.reshape(cells_x, cells_y, slots, area)  6.69 us
    reshape x1, local copies, waits for them, and re-layouts, body(): left_blocks.reshape(rows * slots, BS, BS)  5.71 us
    reshape x1, local copies, waits for them, and re-layouts, body(): right_blocks.reshape(rows * slots, BS, BS)  4.13 us

profile of v5, /device:TPU:0, one launch (start us, length us, event | category | flops | bytes accessed | tf_op | source)
XLA Modules:
  0.0 154.1 jit_solution(1838897527088185713)
XLA Ops:
  0.0 0.0 copy-start
  0.0 1.4 pad.4.targets
  1.4 0.8 fusion.16
  2.3 0.3 convert_reduce_fusion
  2.6 0.4 select_reduce_fusion
  2.9 0.7 reshape.61.turn_of
  3.6 0.7 reshape.60.place
  4.3 0.7 broadcast_in_dim.45.codes
  5.0 5.7 %reshape.63.left = bf16[128,96,96]{2,1,0:T(8,128)(2,1)} reshape(bf16[2,4,16,9216]{3,2,1,0:T(8,128)(2,1)} %param.5) | data formatting | bytes 4718592 | tf_op jit(solution)/shard_map/reshape | solution.py:331
  10.7 0.0 copy-done
  10.7 4.1 %reshape.62.tiles = bf16[128,96,96]{2,1,0:T(8,128)(2,1)} reshape(bf16[2,4,16,9216]{3,2,1,0:T(8,128)(2,1)S(1)} %copy-done) | data formatting | bytes 4718592 | tf_op jit(solution)/shard_map/reshape | solution.py:330
  14.8 132.5 %shard_map.55 = bf16[8,16,96,96]{3,2,1,0:T(8,128)(2,1)} custom-call(s32[128]{0:T(128)} %reshape.60.place, s32[128]{0:T(128)} %reshape.61.turn_of, bf16[128,96,96]{2,1,0:T(8,128)(2,1)} %reshape.62.tiles, bf16[128,96,96]{2,1,0:T(8,128)(2,1)} %reshape.63.left, s32[2,4,16,128]{3,2,1,0:T(8,128)} %broadcast_in_dim.45.codes, s32[8,1,128]{2,1,0:T(1,128)} %pad.4.targets), custom_call_target="tpu_custom_call" | custom-call | flops 3623878656 | bytes 7077888 | tf_op jit(solution)/shard_map/pallas_call | solution.py:298
  147.4 6.7 %reshape.65 = bf16[2,4,16,9216]{3,2,1,0:T(8,128)(2,1)} reshape(bf16[8,16,96,96]{3,2,1,0:T(8,128)(2,1)} %shard_map.55) | data formatting | bytes 4718592 | tf_op jit(solution)/shard_map/reshape | solution.py:335
  (6 shorter events, 0.0 us)
Async XLA Ops:
  0.0 10.7 %copy-start = (bf16[2,4,16,9216]{3,2,1,0:T(8,128)(2,1)S(1)}, bf16[2,4,16,9216]{3,2,1,0:T(8,128)(2,1)}, u32[]{:S(2)}) copy-start(bf16[2,4,16,9216]{3,2,1,0:T(8,128)(2,1)} %param.6) | copy-start | bytes 7077892
